TPU v7x, 128 devices: a whole 4x4x4 slice. The times are simulated.
128 devices in a mesh: dp: 32 (over y, x, core), mp: 4 (over z).
Axes of the slice: x: 4, y: 4, z: 4, core: 2. Of those that a mesh axis runs over, the one named last changes fastest.
Arguments:
- hidden: bfloat16 [1024, 8192], P('dp', 'mp'), may hold values from -6 to 6
- base_query_projection: bfloat16 [1024, 8192], P('dp', 'mp'), may hold values from -240 to 240
- adapter_owner_map: int32 [1024, 1], P('dp'), may hold values from 0 to 31; in each aligned block of 32 rows (0 to 31, 32 to 63, ...) at most 2 rows name the same one
- adapter_fetch_table: int32 [32, 32], P('dp'), may hold values from 0 to 3
- adapter_down_panels: bfloat16 [128, 64, 8192], P('dp', None, 'mp'), may hold values from -0.0625 to 0.0625
- adapter_up_panels: bfloat16 [128, 64, 8192], P('dp', None, 'mp'), may hold values from -0.75 to 0.75
- key_value_page_cache: bfloat16 [4096, 2, 128, 1024], P('dp', None, None, 'mp'), may hold values from -6 to 6
- request_page_table: int32 [1024, 4], P('dp'), may hold values from 0 to 159, as said below
- page_transfer_table: int32 [32, 32], P('dp'), may hold values from 0 to 127
- page_entry_mask: int32 [1024, 4], P('dp'), may hold values 0 or 1
- lengths: int32 [1024], P('dp'), may hold values from 1 to 512
- fresh_key_value: bfloat16 [1024, 2, 1024], P('dp', None, 'mp'), may hold values from -6 to 6
Outputs:
- attended: bfloat16 [1024, 8192], P('dp', 'mp')
Inputs may be any that keep to these rules, and one draw needn't show every extreme that they name: `adapter_owner_map`: within each aligned block of 32 rows no owner is named by more than 2 rows, a bound that some block reaches. `request_page_table`: on each device the entries below 128 are distinct; an entry 128 + p stands at most once on a device and names the page listed in that device's row of page_transfer_table for owner p.
All inputs are finite; a program needn't handle non-finite values. No bound on the sum of `page_entry_mask` on one device may be relied on, other than what follows from the above.
Results may differ from a plain program's by a relative error of at most 0.025.
Values may be sent and summed in bfloat16 or wider, within the bound.
A program may use at most 192 MiB of HBM per device.

v0:
```python
import math

import jax
import jax.numpy as jnp
from jax import lax
from jax.sharding import PartitionSpec as P

HD = 128
MAXP = 4


adapter_scale = 2.0
masked_score = -1e30


def softmax_parts(scores, usable):
    scores = jnp.where(usable, scores, masked_score)
    highest = jnp.max(scores, axis=-1)
    weights = jnp.where(usable, jnp.exp(scores - highest[..., None]), 0.0)
    return (highest, jnp.sum(weights, axis=-1), weights.astype(jnp.bfloat16))


def shards(
    hidden,
    base_query_projection,
    adapter_owner_map,
    adapter_fetch_table,
    adapter_down_panels,
    adapter_up_panels,
    key_value_page_cache,
    request_page_table,
    page_transfer_table,
    page_entry_mask,
    lengths,
    fresh_key_value,
):
    peer_count = lax.axis_size("dp")
    rows_here = hidden.shape[0]
    page_len = key_value_page_cache.shape[2]
    kv_width = key_value_page_cache.shape[3]
    kv_heads = kv_width // HD
    q_width = base_query_projection.shape[1]
    group_size = q_width // kv_width
    adapter_rank_size = adapter_down_panels.shape[1]
    root_size = math.sqrt(HD)
    requested_adapter, wanted_page = (
        lax.all_to_all(adapter_fetch_table, "dp", split_axis=1, concat_axis=0, tiled=True),
        lax.all_to_all(page_transfer_table, "dp", split_axis=1, concat_axis=0, tiled=True),
    )
    peer_ids = jnp.arange(peer_count, dtype=jnp.int32)
    owner_hot = adapter_owner_map[:, 0][:, None] == peer_ids[None, :]
    selected_down_panel = adapter_down_panels[requested_adapter[:, 0]]
    selected_up_panel = adapter_up_panels[requested_adapter[:, 0]]
    got_down, got_up = (
        lax.all_to_all(selected_down_panel, "dp", split_axis=0, concat_axis=0, tiled=True),
        lax.all_to_all(selected_up_panel, "dp", split_axis=0, concat_axis=0, tiled=True),
    )
    projected = jnp.einsum("rd,pkd->rpk", hidden, got_down, preferred_element_type=jnp.float32)
    partial_rank = jnp.sum(projected * owner_hot[:, :, None].astype(jnp.float32), axis=1)
    reduced = lax.psum(partial_rank, "mp").astype(jnp.bfloat16)
    spread = (reduced[:, None, :] * owner_hot[:, :, None].astype(jnp.bfloat16)).reshape(
        rows_here, peer_count * adapter_rank_size
    )
    query_update = jnp.dot(
        spread,
        got_up.reshape(peer_count * adapter_rank_size, q_width),
        preferred_element_type=jnp.float32,
    ).astype(jnp.bfloat16)
    adapted_query = (
        base_query_projection.astype(jnp.float32) + adapter_scale * query_update.astype(jnp.float32)
    ).astype(jnp.bfloat16)
    query_heads = adapted_query.reshape(rows_here, kv_heads, group_size, HD)
    token_ids = jnp.arange(MAXP * page_len)
    live = (page_entry_mask[:, token_ids // page_len] == 1) & (
        token_ids[None, :] < lengths[:, None]
    )
    fresh_keys = fresh_key_value[:, 0].reshape(rows_here, 1, kv_heads, HD)
    fresh_values = fresh_key_value[:, 1].reshape(rows_here, 1, kv_heads, HD)
    chosen_pages = key_value_page_cache[wanted_page[:, 0]]
    arrived = lax.all_to_all(chosen_pages, "dp", split_axis=0, concat_axis=0, tiled=True)
    extended = jnp.concatenate([key_value_page_cache, arrived], 0)
    cache = extended[request_page_table]
    usable = live
    keys = jnp.concatenate(
        [cache[:, :, 0].reshape(rows_here, MAXP * page_len, kv_heads, HD), fresh_keys], 1
    )
    values = jnp.concatenate(
        [cache[:, :, 1].reshape(rows_here, MAXP * page_len, kv_heads, HD), fresh_values], 1
    )
    usable = jnp.concatenate([usable, jnp.ones((rows_here, 1), bool)], 1)
    scores = (
        jnp.einsum("rgqd,rtgd->rgqt", query_heads, keys, preferred_element_type=jnp.float32)
        / root_size
    )
    highest, total, weights = softmax_parts(scores, usable[:, None, None, :])
    summed = jnp.einsum("rgqt,rtgd->rgqd", weights, values, preferred_element_type=jnp.float32)
    highest, total, summed = (highest, total, summed)
    attended = summed / total[..., None]
    return attended.reshape(rows_here, q_width).astype(jnp.bfloat16)


def solution(mesh):
    return jax.shard_map(
        shards,
        mesh=mesh,
        in_specs=(
            P("dp", "mp"),
            P("dp", "mp"),
            P("dp", None),
            P("dp", None),
            P("dp", None, "mp"),
            P("dp", None, "mp"),
            P("dp", None, None, "mp"),
            P("dp", None),
            P("dp", None),
            P("dp", None),
            P("dp"),
            P("dp", None, "mp"),
        ),
        out_specs=P("dp", "mp"),
        check_vma=False,
    )
```

profile of v0, /device:TPU:1, one launch (start us, length us, event | category | flops | bytes accessed | tf_op | source)
XLA Modules:
  0.0 337.3 jit_solution(15165035266097317866)
XLA Ops:
  0.0 1.4 copy.31
  1.4 8.6 %all-to-all-start.3 = ((s32[1,32,1]{2,0,1:T(1,128)}), s32[1,32,1]{2,0,1:T(1,128)S(1)}, u32[]{:S(2)}, u32[]{:S(2)}) async-start(s32[1,32,1]{2,0,1:T(1,128)} %copy.31), calls=%async_computation.3 | async-start | bytes 32768 | tf_op jit(solution)/shard_map/all_to_all | solution.py:48
  10.0 1.3 copy.30
  11.4 5.5 %all-to-all-done.3 = s32[1,32,1]{2,0,1:T(1,128)S(1)} async-done(((s32[1,32,1]{2,0,1:T(1,128)}), s32[1,32,1]{2,0,1:T(1,128)S(1)}, u32[]{:S(2)}, u32[]{:S(2)}) %all-to-all-start.3) | async-done | bytes 160 | tf_op jit(solution)/shard_map/all_to_all | solution.py:48
  16.9 4.2 %all-to-all-start = ((s32[1,32,1]{2,0,1:T(1,128)}), s32[1,32,1]{2,0,1:T(1,128)S(1)}, u32[]{:S(2)}, u32[]{:S(2)}) async-start(s32[1,32,1]{2,0,1:T(1,128)} %copy.30), calls=%async_computation | async-start | bytes 32768 | tf_op jit(solution)/shard_map/all_to_all | solution.py:47
  21.1 0.7 reduce.1
  21.7 8.6 %gather_fusion.3 = bf16[32,2,128,256]{3,2,1,0:T(8,128)(2,1)} fusion(bf16[128,2,128,256]{3,2,1,0:T(8,128)(2,1)} %param.18, s32[1024]{0:T(1024)S(1)} %pad_clamp_fusion.1), kind=kCustom, calls=%fused_computation.3 | custom fusion | bytes 8388736 | tf_op jit(solution)/shard_map/gather | solution.py:79
  30.3 7.5 %all-to-all-start.4 = ((bf16[32,2,128,256]{3,2,1,0:T(8,128)(2,1)}), bf16[32,2,128,256]{3,2,1,0:T(8,128)(2,1)}, u32[]{:S(2)}, u32[]{:S(2)}) async-start(bf16[32,2,128,256]{3,2,1,0:T(8,128)(2,1)} %gather_fusion.3), calls=%async_computation.4 | async-start | bytes 8388608 | tf_op jit(solution)/shard_map/all_to_all | solution.py:80
  37.8 0.7 reduce
  38.5 5.0 %gather_fusion.1 = bf16[32,64,2048]{2,1,0:T(8,128)(2,1)} fusion(bf16[4,64,2048]{2,1,0:T(8,128)(2,1)S(1)} %copy-done, s32[1024]{0:T(1024)S(1)} %pad_clamp_fusion.2), kind=kCustom, calls=%fused_computation.1 | custom fusion | bytes 16777344 | tf_op jit(solution)/shard_map/gather | solution.py:52
  43.5 44.6 %all-to-all-done.4 = bf16[32,2,128,256]{3,2,1,0:T(8,128)(2,1)} async-done(((bf16[32,2,128,256]{3,2,1,0:T(8,128)(2,1)}), bf16[32,2,128,256]{3,2,1,0:T(8,128)(2,1)}, u32[]{:S(2)}, u32[]{:S(2)}) %all-to-all-start.4) | async-done | bytes 4194336 | tf_op jit(solution)/shard_map/all_to_all | solution.py:80
  88.1 8.1 %all-to-all-start.1 = ((bf16[32,64,2048]{2,1,0:T(8,128)(2,1)}), bf16[32,64,2048]{2,1,0:T(8,128)(2,1)}, u32[]{:S(2)}, u32[]{:S(2)}) async-start(bf16[32,64,2048]{2,1,0:T(8,128)(2,1)} %gather_fusion.1), calls=%async_computation.1 | async-start | bytes 16777216 | tf_op jit(solution)/shard_map/all_to_all | solution.py:55
  96.2 5.1 %gather_fusion.2 = bf16[32,64,2048]{2,1,0:T(8,128)(2,1)} fusion(bf16[4,64,2048]{2,1,0:T(8,128)(2,1)S(1)} %copy-done.3, s32[1024]{0:T(1024)S(1)} %pad_clamp_fusion.2), kind=kCustom, calls=%fused_computation.2 | custom fusion | bytes 16777344 | tf_op jit(solution)/shard_map/gather | solution.py:53
  101.3 94.7 %all-to-all-done.1 = bf16[32,64,2048]{2,1,0:T(8,128)(2,1)} async-done(((bf16[32,64,2048]{2,1,0:T(8,128)(2,1)}), bf16[32,64,2048]{2,1,0:T(8,128)(2,1)}, u32[]{:S(2)}, u32[]{:S(2)}) %all-to-all-start.1) | async-done | bytes 8388640 | tf_op jit(solution)/shard_map/all_to_all | solution.py:55
  196.0 11.1 %all-to-all-start.2 = ((bf16[32,64,2048]{2,1,0:T(8,128)(2,1)}), bf16[32,64,2048]{2,1,0:T(8,128)(2,1)}, u32[]{:S(2)}, u32[]{:S(2)}) async-start(bf16[32,64,2048]{2,1,0:T(8,128)(2,1)} %gather_fusion.2), calls=%async_computation.2 | async-start | bytes 16777216 | tf_op jit(solution)/shard_map/all_to_all | solution.py:56
  207.1 0.1 copy.32
  207.2 0.1 reshape.206
  207.3 1.0 gather_fusion
  208.4 0.1 copy.39
  208.7 19.9 %pad_maximum_fusion = bf16[160,2,128,256]{3,2,1,0:T(8,128)(2,1)} fusion(bf16[32,2,128,256]{3,2,1,0:T(8,128)(2,1)} %all-to-all-done.4, bf16[128,2,128,256]{3,2,1,0:T(8,128)(2,1)} %param.18), kind=kLoop, calls=%fused_computation.6 | loop fusion | flops 10485760 | bytes 41943040 | tf_op jit(solution)/shard_map/concatenate | solution.py:81
  228.6 15.4 %gather_fusion.4 = bf16[128,2,128,256]{3,2,1,0:T(8,128)(2,1)} fusion(bf16[160,2,128,256]{3,2,1,0:T(8,128)(2,1)} %pad_maximum_fusion, s32[1024]{0:T(1024)S(1)} %pad_clamp_fusion), kind=kCustom, calls=%fused_computation.4 | custom fusion | bytes 33554944 | tf_op jit(solution)/shard_map/gather | solution.py:82
  244.0 11.7 %slice_bitcast_fusion.1 = (bf16[32,4,1,128,256]{4,3,1,0,2:T(8,128)(2,1)}, bf16[32,4,1,128,256]{4,3,1,0,2:T(8,128)(2,1)}) fusion(bf16[32,4,2,128,256]{4,3,2,1,0:T(8,128)(2,1)} %bitcast.67), kind=kLoop, calls=%fused_computation.16 | loop fusion | bytes 33554432
  255.7 12.6 %reshape_squeeze.12 = bf16[32,512,2,128]{3,2,1,0:T(2,128)(2,1)} reshape(bf16[32,4,1,128,256]{4,3,1,0,2:T(8,128)(2,1)} %get-tuple-element.5) | data formatting | bytes 16777216 | tf_op jit(solution)/shard_map/reshape;squeeze | solution.py:85
  268.3 8.8 %copy.34 = bf16[32,512,2,128]{3,1,2,0:T(8,128)(2,1)} copy(bf16[32,512,2,128]{3,2,1,0:T(2,128)(2,1)} %reshape_squeeze.12) | data formatting | bytes 16777216 | tf_op jit(solution)/shard_map/reshape;squeeze | solution.py:85
  277.1 12.6 %reshape_squeeze.14 = bf16[32,512,2,128]{3,2,1,0:T(2,128)(2,1)} reshape(bf16[32,4,1,128,256]{4,3,1,0,2:T(8,128)(2,1)} %get-tuple-element.6) | data formatting | bytes 16777216 | tf_op jit(solution)/shard_map/reshape;squeeze | solution.py:88
  289.7 8.8 %copy.36 = bf16[32,512,2,128]{3,1,2,0:T(8,128)(2,1)} copy(bf16[32,512,2,128]{3,2,1,0:T(2,128)(2,1)} %reshape_squeeze.14) | data formatting | bytes 16777216 | tf_op jit(solution)/shard_map/reshape;squeeze | solution.py:88
  298.5 7.4 %fusion.24 = f32[32,64]{1,0:T(8,128)S(1)} fusion(bf16[32,64,2048]{2,1,0:T(8,128)(2,1)} %all-to-all-done.1, f32[32,32]{0,1:T(8,128)S(1)} %get-tuple-element.9, bf16[32,2048]{1,0:T(8,128)(2,1)S(1)} %copy-done.4), kind=kOutput, calls=%fused_computation.30 | convolution fusion | flops 268564480 | bytes 8531968 | tf_op jit(solution)/shard_map/rd,pkd->rpk/dot_general | solution.py:58
  305.9 14.9 %psum.7 = bf16[32,64]{1,0:T(8,128)(2,1)S(1)} all-reduce(f32[32,64]{1,0:T(8,128)S(1)} %fusion.24), channel_id=1, replica_groups=mesh['dp'=32,'mp'=4] {'mp'}, use_global_device_ids=true, to_apply=%region_1.0 | all-reduce | flops 2048 | bytes 12288 | tf_op jit(solution)/shard_map/psum | solution.py:60
  320.7 5.1 %fusion.25 = bf16[4,8,16,128]{3,1,2,0:T(8,128)(2,1)S(1)} fusion(bf16[32,64,2048]{2,1,0:T(8,128)(2,1)} %all-to-all-done.2, bf16[32,2048]{1,0:T(8,128)(2,1)S(1)} %copy-done.5, bf16[32,32]{0,1:T(8,128)(2,1)S(1)} %get-tuple-element.10, bf16[32,64]{1,0:T(8,128)(2,1)S(1)} %psum.7), kind=kOutput, calls=%fused_computation.31 | convolution fusion | flops 268894208 | bytes 8656896 | tf_op jit(solution)/shard_map/dot_general | solution.py:64
  325.9 6.0 %fusion.44 = (f32[32,2,8]{2,1,0:T(2,128)S(1)}, bf16[32,2,8,513]{3,2,1,0:T(8,128)(2,1)S(1)}) fusion(pred[32,513]{1,0:T(8,128)(4,1)S(1)} %concatenate.12.clone, bf16[32,2,8,128]{3,2,1,0:T(8,128)(2,1)S(1)} %bitcast.68, bf16[32,1,2,128]{3,1,2,0:T(2,128)(2,1)S(1)} %get-tuple-element.7, bf16[32,512,2,128]{3,1,2,0:T(8,128)(2,1)} %copy.34), kind=kOutput, calls=%fused_computation.63 | convolution fusion | flops 85626368 | bytes 9079840 | tf_op jit(solution)/shard_map/sub | solution.py:19
  331.9 4.8 %fusion.29 = bf16[32,2,8,128]{3,2,1,0:T(8,128)(2,1)S(1)} fusion(bf16[32,1,2,128]{3,1,2,0:T(2,128)(2,1)S(1)} %get-tuple-element.8, bf16[32,512,2,128]{3,1,2,0:T(8,128)(2,1)} %copy.36, bf16[32,2,8,513]{3,2,1,0:T(8,128)(2,1)S(1)} %get-tuple-element.12, f32[32,2,8]{2,1,0:T(2,128)S(1)} %get-tuple-element.11), kind=kOutput, calls=%fused_computation.33 | convolution fusion | flops 84180992 | bytes 9063424 | tf_op jit(solution)/shard_map/rgqt,rtgd->rgqd/dot_general | solution.py:96
  336.6 0.7 copy.43
  (35 shorter events, 0.2 us)
Async XLA Ops:
  0.0 38.5 %copy-start = (bf16[4,64,2048]{2,1,0:T(8,128)(2,1)S(1)}, bf16[4,64,2048]{2,1,0:T(8,128)(2,1)}, u32[]{:S(2)}) copy-start(bf16[4,64,2048]{2,1,0:T(8,128)(2,1)} %param.16) | copy-start | bytes 3145732
  1.4 15.5 %all-to-all-start.3 = ((s32[1,32,1]{2,0,1:T(1,128)}), s32[1,32,1]{2,0,1:T(1,128)S(1)}, u32[]{:S(2)}, u32[]{:S(2)}) async-start(s32[1,32,1]{2,0,1:T(1,128)} %copy.31), calls=%async_computation.3 | async-start | bytes 32768 | tf_op jit(solution)/shard_map/all_to_all | solution.py:48
  16.9 13.4 %all-to-all-start = ((s32[1,32,1]{2,0,1:T(1,128)}), s32[1,32,1]{2,0,1:T(1,128)S(1)}, u32[]{:S(2)}, u32[]{:S(2)}) async-start(s32[1,32,1]{2,0,1:T(1,128)} %copy.30), calls=%async_computation | async-start | bytes 32768 | tf_op jit(solution)/shard_map/all_to_all | solution.py:47
  30.3 57.8 %all-to-all-start.4 = ((bf16[32,2,128,256]{3,2,1,0:T(8,128)(2,1)}), bf16[32,2,128,256]{3,2,1,0:T(8,128)(2,1)}, u32[]{:S(2)}, u32[]{:S(2)}) async-start(bf16[32,2,128,256]{3,2,1,0:T(8,128)(2,1)} %gather_fusion.3), calls=%async_computation.4 | async-start | bytes 8388608 | tf_op jit(solution)/shard_map/all_to_all | solution.py:80
  43.5 52.6 %copy-start.3 = (bf16[4,64,2048]{2,1,0:T(8,128)(2,1)S(1)}, bf16[4,64,2048]{2,1,0:T(8,128)(2,1)}, u32[]{:S(2)}) copy-start(bf16[4,64,2048]{2,1,0:T(8,128)(2,1)} %param.17) | copy-start | bytes 3145732
  88.1 107.9 %all-to-all-start.1 = ((bf16[32,64,2048]{2,1,0:T(8,128)(2,1)}), bf16[32,64,2048]{2,1,0:T(8,128)(2,1)}, u32[]{:S(2)}, u32[]{:S(2)}) async-start(bf16[32,64,2048]{2,1,0:T(8,128)(2,1)} %gather_fusion.1), calls=%async_computation.1 | async-start | bytes 16777216 | tf_op jit(solution)/shard_map/all_to_all | solution.py:55
  101.3 105.8 %copy-start.7 = (s32[32,4]{0,1:T(4,128)S(1)}, s32[32,4]{0,1:T(4,128)}, u32[]{:S(2)}) copy-start(s32[32,4]{0,1:T(4,128)} %param.19) | copy-start | bytes 1540
  101.3 106.0 %copy-start.2 = (s32[32,4]{0,1:T(4,128)S(1)}, s32[32,4]{0,1:T(4,128)}, u32[]{:S(2)}) copy-start(s32[32,4]{0,1:T(4,128)} %param.21) | copy-start | bytes 1540
  101.3 107.1 %copy-start.8 = (s32[32]{0:T(128)S(1)}, s32[32]{0:T(128)}, u32[]{:S(2)}) copy-start(s32[32]{0:T(128)} %param.22) | copy-start | bytes 388
  101.3 107.3 %copy-start.9 = (s32[32,1]{0,1:T(1,128)S(1)}, s32[32,1]{0,1:T(1,128)}, u32[]{:S(2)}) copy-start(s32[32,1]{0,1:T(1,128)} %param.14) | copy-start | bytes 388
  101.3 107.3 %copy-start.6 = (bf16[32,2,256]{2,1,0:T(2,128)(2,1)S(1)}, bf16[32,2,256]{2,1,0:T(2,128)(2,1)}, u32[]{:S(2)}) copy-start(bf16[32,2,256]{2,1,0:T(2,128)(2,1)} %param.23) | copy-start | bytes 98308
  196.0 124.8 %all-to-all-start.2 = ((bf16[32,64,2048]{2,1,0:T(8,128)(2,1)}), bf16[32,64,2048]{2,1,0:T(8,128)(2,1)}, u32[]{:S(2)}, u32[]{:S(2)}) async-start(bf16[32,64,2048]{2,1,0:T(8,128)(2,1)} %gather_fusion.2), calls=%async_computation.2 | async-start | bytes 16777216 | tf_op jit(solution)/shard_map/all_to_all | solution.py:56
  289.7 8.8 %copy-start.4 = (bf16[32,2048]{1,0:T(8,128)(2,1)S(1)}, bf16[32,2048]{1,0:T(8,128)(2,1)}, u32[]{:S(2)}) copy-start(bf16[32,2048]{1,0:T(8,128)(2,1)} %param.12) | copy-start | bytes 393220
  298.5 22.3 %copy-start.5 = (bf16[32,2048]{1,0:T(8,128)(2,1)S(1)}, bf16[32,2048]{1,0:T(8,128)(2,1)}, u32[]{:S(2)}) copy-start(bf16[32,2048]{1,0:T(8,128)(2,1)} %param.13) | copy-start | bytes 393220
  325.8 11.5 %copy-start.1 = (bf16[4,64,2048]{2,1,0:T(8,128)(2,1)S(1)}, bf16[4,64,2048]{2,1,0:T(8,128)(2,1)}, u32[]{:S(2)}) copy-start(bf16[4,64,2048]{2,1,0:T(8,128)(2,1)} %param.16) | copy-start | bytes 3145732
where the time goes:
time: 341 us; the launch traced here: 337 us
  waiting for transfers between devices  145 us (43%)
  local copies, waits for them, and re-layouts  93.4 us (27%)
  starting transfers between devices  39.4 us (12%)
  matrix products  23.2 us (7%)
  other arithmetic  21.4 us (6%)
  blocking collectives  14.9 us (4%)
    all_to_all x1, waiting for transfers between devices, shards(): lax.all_to_all(selected_down_panel, 'dp', split_axis=0, concat_axis=0, ti...  94.7 us
    all_to_all x1, waiting for transfers between devices, shards(): lax.all_to_all(chosen_pages, 'dp', split_axis=0, concat_axis=0, tiled=True)  44.6 us
    another operation x2, local copies, waits for them, and re-layouts, shards(): cache[:, :, 1].reshape(rows_here, MAXP * page_len, kv_heads, HD)  21.4 us
    another operation x2, local copies, waits for them, and re-layouts, shards(): cache[:, :, 0].reshape(rows_here, MAXP * page_len, kv_heads, HD)  21.4 us
    concatenate x1, other arithmetic, shards(): extended = jnp.concatenate([key_value_page_cache, arrived], 0)  19.9 us
    gather x1, local copies, waits for them, and re-layouts, shards(): cache = extended[request_page_table]  15.4 us
    psum x1, blocking collectives, shards(): reduced = lax.psum(partial_rank, 'mp').astype(jnp.bfloat16)  14.9 us
    unnamed x24, local copies, waits for them, and re-layouts  12.6 us
  transfers between devices with their start and end apart: 5, of which 3 were waited for; matrix products, arithmetic and copies ran while one was open for 36% of the time, Pallas kernels for 0%

commit v1 on v0

v1 whole, which is shorter than its diff:
```python
import functools
import math

import jax
import jax.numpy as jnp
from jax import lax
from jax.experimental import pallas as pl
from jax.experimental.pallas import tpu as pltpu
from jax.sharding import PartitionSpec as P

MESH = pl.DeviceIdType.MESH
BF, F32, I32 = jnp.bfloat16, jnp.float32, jnp.int32

N = 32
Z = 4
HD = 128
HEADS = 16
PAGE = 128
MAXP = 4
RANK = 64
CH = 8
CW = 256
ROWS = N * HEADS
SCALE = 1.0 / math.sqrt(HD)
LOW = -1e30
NT = (((1,), (1,)), ((), ()))


def iota(shape, dim):
    return lax.broadcasted_iota(I32, shape, dim)


def hot(mask):
    return jnp.where(mask, 1.0, 0.0).astype(BF)


def dot(a, b):
    return jnp.dot(a, b, preferred_element_type=F32)


def pieces(x):
    hi = x.astype(BF).astype(F32)
    mid = (x - hi).astype(BF).astype(F32)
    return hi, mid, x - hi - mid


def block_select(left, right, rows):
    low_heads = (iota((rows, 1), 0) & 8) == 0
    return jnp.where(low_heads, left, right)


def kernel(
    own_ref, fetch_ref, tab_ref, move_ref, mask_ref, len_ref, fresh_ref, tab_s,
    hid_hbm, base_hbm, down_hbm, up_hbm, cache_hbm,
    out_ref,
    hid, base, down, up, cache,
    hsend, hrecv, dsend, drecv, tsend, trecv, tsm, zbuf, qsend, qrecv, psend, precv,
    pm, pinv, ph, gm, qsel, ex, cx, st1, st2, tmask,
    qbd, qbs, fkv, sl, wl, ss, ws, ol, loc, locp,
    lsem, ssem, rsem,
):
    d0 = lax.axis_index("dp")
    z0 = lax.axis_index("mp")

    barrier = pltpu.get_barrier_semaphore()

    def greet(k, _):
        pl.semaphore_signal(
            barrier, inc=1, device_id={"dp": lax.rem(d0 + k, N)}, device_id_type=MESH
        )
        return 0

    lax.fori_loop(1, N, greet, 0)
    for k in range(1, Z):
        pl.semaphore_signal(
            barrier, inc=1, device_id={"mp": lax.rem(z0 + k, Z)}, device_id_type=MESH
        )

    cp_hid = pltpu.make_async_copy(hid_hbm, hid, lsem.at[0])
    cp_base = pltpu.make_async_copy(base_hbm, base, lsem.at[1])
    cp_down = pltpu.make_async_copy(down_hbm, down, lsem.at[2])
    cp_up = pltpu.make_async_copy(up_hbm, up, lsem.at[3])
    cp_cache = pltpu.make_async_copy(cache_hbm, cache, lsem.at[4])
    for cp in (cp_hid, cp_down, cp_up, cp_base, cp_cache):
        cp.start()

    def scatter(src, dst, rows, which):
        def body(k, _):
            t = lax.rem(d0 + k, N)
            pltpu.make_async_remote_copy(
                src_ref=src.at[pl.ds(pl.multiple_of(t * rows, rows), rows)],
                dst_ref=dst.at[pl.ds(pl.multiple_of(d0 * rows, rows), rows)],
                send_sem=ssem.at[which],
                recv_sem=rsem.at[which],
                device_id={"dp": t},
                device_id_type=MESH,
            ).start()
            return 0

        lax.fori_loop(1, N, body, 0)

    def drain(ref, rows, sem):
        part = ref.at[pl.ds(0, (N - 1) * rows)]
        pltpu.make_async_copy(part, part, sem).wait()

    def keep(src, dst, rows):
        here = pl.ds(pl.multiple_of(d0 * rows, rows), rows)
        dst[here, :] = src[here, :]

    ri, ci = iota((N, N), 0), iota((N, N), 1)
    rif, cif = ri.astype(F32), ci.astype(F32)

    def column(row):
        return jnp.sum(jnp.where(ri == ci, row, 0.0), axis=1, keepdims=True)

    own_r = own_ref[...].astype(F32)
    own_c = column(own_r)
    same = own_c == own_r
    rank_c = jnp.sum(jnp.where(same & (ci < ri), 1.0, 0.0), axis=1, keepdims=True)
    key_c = own_c * HEADS + rank_c * CH
    length = len_ref[...].astype(F32)
    fetch_c = column(fetch_ref[...].astype(F32))
    move_c = column(move_ref[...].astype(F32))
    req_c = jnp.zeros((N, 1), F32)
    nlp_c = jnp.zeros((N, 1), F32)
    remote = jnp.zeros((N, N), F32)
    local_live = []
    for j in range(MAXP):
        tab_r = tab_ref[j : j + 1, :].astype(F32)
        live_r = jnp.where(
            mask_ref[j : j + 1, :] == 1, jnp.clip(length - PAGE * j, 0.0, PAGE), 0.0
        )
        hit = tab_r == rif + PAGE
        req_c += jnp.sum(jnp.where(hit, cif + 1.0, 0.0), axis=1, keepdims=True)
        nlp_c += jnp.sum(jnp.where(hit, live_r, 0.0), axis=1, keepdims=True)
        local_live.append(column(jnp.where(tab_r < PAGE, live_r, 0.0)))
        remote += jnp.where(column(tab_r) == cif + PAGE, 1.0, 0.0)

    lane = iota((N, 128), 1)
    tsend[...] = jnp.where(
        lane == 0, fetch_c, jnp.where(lane == 1, move_c, jnp.where(lane == 2, nlp_c, 0.0))
    ).astype(I32)

    jj, rr = iota((N, CW), 1), iota((N, CW), 0)
    target = jnp.sum(
        jnp.where(rr == (jj & (N - 1)), key_c, 0.0), axis=0, keepdims=True
    ) + (jj[:1] >> 5).astype(F32)
    place = hot(iota((ROWS, CW), 0).astype(F32) == target)
    cp_hid.wait()
    chunks = jnp.concatenate([hid[:, c * CW : (c + 1) * CW] for c in range(CH)], axis=0)
    hsend[...] = dot(place, chunks).astype(BF)

    pl.semaphore_wait(barrier, N - 1 + Z - 1)
    scatter(hsend, hrecv, HEADS, 0)
    scatter(tsend, trecv, 1, 1)
    keep(hsend, hrecv, HEADS)
    keep(tsend, trecv, 1)

    blk = 64

    def rows_of(b):
        return pl.ds(pl.multiple_of(b * blk, blk), blk)

    vals = jnp.where(lane == 0, req_c, 0.0)
    for j in range(MAXP):
        vals = jnp.where(lane == j + 1, local_live[j], vals)
    tmask[...] = jnp.concatenate([remote, jnp.zeros((N, 128 - N), F32)], axis=1)
    vals = vals.astype(BF)
    for c in range(CH):
        gm[c * N : (c + 1) * N, :] = hot(iota((N, ROWS), 1).astype(F32) == key_c + float(c))

    def build(b, _):
        i = iota((blk, 1), 0) + b * blk
        j = iota((blk, ROWS), 1)
        at = rows_of(b)
        pm[at, :] = hot(j == ((i & 31) << 4) + (((i >> 5) & 1) << 3) + (i >> 6))
        pinv[at, :] = hot(j == ((i & 7) << 6) + (((i >> 3) & 1) << 5) + (i >> 4))
        ph[at, :] = hot(j == ((i & 31) << 4) + (i >> 5))
        head = ((i & 1) << 8) + (((i >> 1) & 7) << 5)
        e = hot(iota((blk, N), 1) == (i >> 4))
        ex[at, :] = e
        x = dot(e, vals)
        cx[at, :] = x
        req = x[:, 0:1]
        qsel[at, :] = hot(
            j.astype(F32) == jnp.where(req > 0.0, req - 1.0 + head.astype(F32), -1.0)
        )
        qsel[pl.ds(pl.multiple_of(ROWS + b * blk, blk), blk), :] = hot(j == head + (i >> 4))
        k0 = dot(hot(iota((blk, 2 * N), 1) == (i >> 4) * 2), fresh_ref[...])
        v0 = dot(hot(iota((blk, 2 * N), 1) == (i >> 4) * 2 + 1), fresh_ref[...])
        fkv[at, :] = jnp.concatenate(
            [
                block_select(k0[:, :HD], k0[:, HD:], blk),
                block_select(v0[:, :HD], v0[:, HD:], blk),
            ],
            axis=1,
        )
        return 0

    lax.fori_loop(0, ROWS // blk, build, 0)

    cp_down.wait()
    drain(trecv, 1, rsem.at[1])
    cp_tsm = pltpu.make_async_copy(trecv, tsm, lsem.at[5])
    cp_tsm.start()
    adapter = trecv[:, 0:1].astype(F32)
    adapter = jnp.concatenate([adapter, adapter], axis=0)
    wanted = (iota((2 * N, CW), 1) >> 6).astype(F32) == adapter
    drain(hrecv, HEADS, rsem.at[0])
    arranged = dot(pm[...], hrecv[...]).astype(BF)
    acc = jnp.zeros((2 * N, CW), F32)
    for c in range(CH):
        acc += lax.dot_general(
            arranged[c * 2 * N : (c + 1) * 2 * N],
            down[:, c * CW : (c + 1) * CW],
            NT,
            preferred_element_type=F32,
        )
    acc = jnp.where(wanted, acc, 0.0)
    zbuf[pl.ds(z0, 1)] = (acc[:, :128] + acc[:, 128:])[None]
    for k in range(1, Z):
        pltpu.make_async_remote_copy(
            src_ref=zbuf.at[z0],
            dst_ref=zbuf.at[z0],
            send_sem=ssem.at[2],
            recv_sem=rsem.at[2],
            device_id={"mp": lax.rem(z0 + k, Z)},
            device_id_type=MESH,
        ).start()
    zpart = zbuf.at[pl.ds(0, Z - 1)]
    cp_up.wait()
    pltpu.make_async_copy(zpart, zpart, rsem.at[2]).wait()
    u = (zbuf[0] + zbuf[1]) + (zbuf[2] + zbuf[3])
    u = jnp.where(wanted, jnp.concatenate([u, u], axis=1), 0.0).astype(BF)
    for c in range(CH):
        st1[c * 2 * N : (c + 1) * 2 * N, :] = dot(u, up[:, c * CW : (c + 1) * CW]).astype(BF)
    dsend[...] = dot(pinv[...], st1[...]).astype(BF)
    scatter(dsend, drecv, HEADS, 3)
    keep(dsend, drecv, HEADS)

    cp_base.wait()
    drain(drecv, HEADS, rsem.at[3])
    base_re = jnp.concatenate([base[:, c * CW : (c + 1) * CW] for c in range(CH)], axis=0)
    query = (base_re.astype(F32) + 2.0 * dot(gm[...], drecv[...])).astype(BF)
    st2[: CW, :] = query[:, :HD]
    st2[CW :, :] = query[:, HD:]
    qsend[...] = dot(qsel[:ROWS, :], st2[...]).astype(BF)
    scatter(qsend, qrecv, HEADS, 4)
    keep(qsend, qrecv, HEADS)
    query = dot(qsel[ROWS:, :], st2[...])
    qbd[:, :HD] = block_select(query, 0.0, ROWS).astype(BF)
    qbd[:, HD:] = block_select(0.0, query, ROWS).astype(BF)
    loc[:, 0:1] = jnp.sum(query * fkv[:, :HD], axis=1, keepdims=True) * SCALE

    cp_cache.wait()

    def local_scores(r, _):
        at = pl.ds(pl.multiple_of(r * HEADS, HEADS), HEADS)
        q = qbd[at, :]
        for j in range(MAXP):
            page = jnp.minimum(tab_s[j, r], PAGE - 1)
            sl[at, j * PAGE : (j + 1) * PAGE] = lax.dot_general(
                q, cache[page, 0], NT, preferred_element_type=F32
            )
        return 0

    lax.fori_loop(0, N, local_scores, 0, unroll=2)

    drain(qrecv, HEADS, rsem.at[4])
    cp_tsm.wait()
    got = qrecv[...].astype(F32)
    qbs[:, :HD] = block_select(got, 0.0, ROWS).astype(BF)
    qbs[:, HD:] = block_select(0.0, got, ROWS).astype(BF)

    def served_scores(d, _):
        at = pl.ds(pl.multiple_of(d * HEADS, HEADS), HEADS)
        page = jnp.clip(tsm[d, 1], 0, PAGE - 1)
        ss[at, :] = lax.dot_general(qbs[at, :], cache[page, 0], NT, preferred_element_type=F32)
        return 0

    lax.fori_loop(0, N, served_scores, 0, unroll=4)
    counts = trecv[...].astype(F32).astype(BF)

    def served_weights(b, _):
        at = rows_of(b)
        n_live = dot(ex[at, :], counts)[:, 2:3]
        live = iota((blk, PAGE), 1).astype(F32) < n_live
        s = jnp.where(live, ss[at, :] * SCALE, LOW)
        m = jnp.max(s, axis=1, keepdims=True)
        w = jnp.where(live, jnp.exp(s - m), 0.0)
        total = jnp.sum(w, axis=1, keepdims=True)
        ws[at, :] = w.astype(BF)
        some = total > 0.0
        total = jnp.where(some, total, 1.0)
        hi, mid, lo = pieces(jnp.where(some, m + jnp.log(total), LOW))
        at_lane = iota((blk, 128), 1)
        stat = jnp.where(at_lane == d0, hi, 0.0)
        stat = jnp.where(at_lane == d0 + N, mid, stat)
        stat = jnp.where(at_lane == d0 + 2 * N, lo, stat)
        psend[at, HD:] = stat.astype(BF)
        ss[at, :] = jnp.broadcast_to(1.0 / total, (blk, 128))
        return 0

    lax.fori_loop(0, ROWS // blk, served_weights, 0)

    def served_values(d, _):
        at = pl.ds(pl.multiple_of(d * HEADS, HEADS), HEADS)
        page = jnp.clip(tsm[d, 1], 0, PAGE - 1)
        o = dot(ws[at, :], cache[page, 1])
        psend[at, :HD] = (block_select(o[:, :HD], o[:, HD:], HEADS) * ss[at, :]).astype(BF)
        return 0

    lax.fori_loop(0, N, served_values, 0, unroll=4)
    scatter(psend, precv, HEADS, 5)
    keep(psend, precv, HEADS)

    def local_weights(b, _):
        at = rows_of(b)
        x = cx[at, :]
        fresh = loc[at, 0:1]
        t = iota((blk, PAGE), 1).astype(F32)
        parts, lives = [], []
        m = fresh
        for j in range(MAXP):
            live = t < x[:, j + 1 : j + 2]
            s = jnp.where(live, sl[at, j * PAGE : (j + 1) * PAGE] * SCALE, LOW)
            m = jnp.maximum(m, jnp.max(s, axis=1, keepdims=True))
            parts.append(s)
            lives.append(live)
        wf = jnp.exp(fresh - m)
        total = wf
        for j in range(MAXP):
            w = jnp.where(lives[j], jnp.exp(parts[j] - m), 0.0)
            total += jnp.sum(w, axis=1, keepdims=True)
            wl[at, j * PAGE : (j + 1) * PAGE] = w.astype(BF)
        at_lane = iota((blk, 128), 1)
        stat = jnp.where(at_lane == 0, m, jnp.where(at_lane == 1, total, 0.0))
        loc[at, :] = jnp.where(at_lane == 2, wf, stat)
        return 0

    lax.fori_loop(0, ROWS // blk, local_weights, 0)

    def local_values(r, _):
        at = pl.ds(pl.multiple_of(r * HEADS, HEADS), HEADS)
        o = jnp.zeros((HEADS, CW), F32)
        for j in range(MAXP):
            page = jnp.minimum(tab_s[j, r], PAGE - 1)
            o += dot(wl[at, j * PAGE : (j + 1) * PAGE], cache[page, 1])
        ol[at, :] = block_select(o[:, :HD], o[:, HD:], HEADS)
        return 0

    lax.fori_loop(0, N, local_values, 0, unroll=2)

    def local_part(b, _):
        at = rows_of(b)
        st = loc[at, :]
        m, total, wf = st[:, 0:1], st[:, 1:2], st[:, 2:3].astype(BF).astype(F32)
        o = (ol[at, :] + wf * fkv[at, HD:]) / total
        hi, mid, lo = pieces(m + jnp.log(total))
        at_lane = iota((blk, 128), 1)
        stat = jnp.where(at_lane == 0, hi, jnp.where(at_lane == 1, mid, 0.0))
        stat = jnp.where(at_lane == 2, lo, stat)
        locp[at, :HD] = o.astype(BF)
        locp[at, HD:] = stat.astype(BF)
        return 0

    lax.fori_loop(0, ROWS // blk, local_part, 0)
    mine = dot(ph[...], locp[...])
    ol[...] = mine[:, :HD]
    loc[...] = mine[:, HD:]

    drain(precv, HEADS, rsem.at[5])
    stats = jnp.zeros((HEADS, 128), F32)
    for p in range(N):
        stats += precv[p * HEADS : (p + 1) * HEADS, HD:].astype(F32)
    stats = stats[:, :N] + stats[:, N : 2 * N] + stats[:, 2 * N : 3 * N]
    reads = tmask[:, :N] > 0.0
    spread = hot(iota((N, ROWS), 0) == (iota((N, ROWS), 1) >> 4))
    lane_head = iota((N, ROWS), 1) & 15
    others = precv[:, :HD]
    for h in range(HEADS):
        at = slice(h * N, (h + 1) * N)
        lse = jnp.where(reads, jnp.broadcast_to(stats[h : h + 1, :], (N, N)), LOW)
        mst = loc[at, :]
        mine = mst[:, 0:1] + mst[:, 1:2] + mst[:, 2:3]
        top = jnp.maximum(jnp.max(lse, axis=1, keepdims=True), mine)
        w = jnp.where(reads, jnp.exp(lse - top), 0.0)
        wm = jnp.exp(mine - top)
        inv = 1.0 / (jnp.sum(w, axis=1, keepdims=True) + wm)
        wide = dot((w * inv).astype(BF), spread)
        wide = jnp.where(lane_head == h, wide, 0.0).astype(BF)
        o = dot(wide, others) + (wm * inv) * ol[at, :]
        out_ref[:, h * HD : (h + 1) * HD] = o.astype(BF)

    drain(hsend, HEADS, ssem.at[0])
    drain(tsend, 1, ssem.at[1])
    pltpu.make_async_copy(zpart, zpart, ssem.at[2]).wait()
    drain(dsend, HEADS, ssem.at[3])
    drain(qsend, HEADS, ssem.at[4])
    drain(psend, HEADS, ssem.at[5])


def shards(
    hidden,
    base_query_projection,
    adapter_owner_map,
    adapter_fetch_table,
    adapter_down_panels,
    adapter_up_panels,
    key_value_page_cache,
    request_page_table,
    page_transfer_table,
    page_entry_mask,
    lengths,
    fresh_key_value,
):
    width = N * 64
    table = request_page_table.T
    vmem = pl.BlockSpec(memory_space=pltpu.VMEM)
    smem = pl.BlockSpec(memory_space=pltpu.SMEM)
    hbm = pl.BlockSpec(memory_space=pl.ANY)
    v = pltpu.VMEM
    return pl.pallas_call(
        kernel,
        out_shape=jax.ShapeDtypeStruct((N, width), BF),
        in_specs=[vmem] * 7 + [smem] + [hbm] * 5,
        out_specs=vmem,
        scratch_shapes=[
            v((N, width), BF),
            v((N, width), BF),
            v((CW, width), BF),
            v((CW, width), BF),
            v((PAGE, 2, PAGE, CW), BF),
            v((ROWS, CW), BF),
            v((ROWS, CW), BF),
            v((ROWS, CW), BF),
            v((ROWS, CW), BF),
            v((N, 128), I32),
            v((N, 128), I32),
            pltpu.SMEM((N, 128), I32),
            v((Z, 2 * N, 128), F32),
            v((ROWS, HD), BF),
            v((ROWS, HD), BF),
            v((ROWS, CW), BF),
            v((ROWS, CW), BF),
            v((ROWS, ROWS), BF),
            v((ROWS, ROWS), BF),
            v((ROWS, ROWS), BF),
            v((CW, ROWS), BF),
            v((2 * ROWS, ROWS), BF),
            v((ROWS, N), BF),
            v((ROWS, 128), F32),
            v((ROWS, CW), BF),
            v((ROWS, HD), BF),
            v((N, 128), F32),
            v((ROWS, CW), BF),
            v((ROWS, CW), BF),
            v((ROWS, CW), F32),
            v((ROWS, ROWS), F32),
            v((ROWS, ROWS), BF),
            v((ROWS, PAGE), F32),
            v((ROWS, PAGE), BF),
            v((ROWS, HD), F32),
            v((ROWS, 128), F32),
            v((ROWS, CW), BF),
            pltpu.SemaphoreType.DMA((6,)),
            pltpu.SemaphoreType.DMA((6,)),
            pltpu.SemaphoreType.DMA((6,)),
        ],
        compiler_params=pltpu.CompilerParams(
            collective_id=0, has_side_effects=True, vmem_limit_bytes=50 * 1024 * 1024
        ),
    )(
        adapter_owner_map.T,
        adapter_fetch_table,
        table,
        page_transfer_table,
        page_entry_mask.T,
        lengths.reshape(1, N),
        fresh_key_value.reshape(2 * N, CW),
        table,
        hidden,
        base_query_projection,
        adapter_down_panels.reshape(CW, width),
        adapter_up_panels.reshape(CW, width),
        key_value_page_cache,
    )


def solution(mesh):
    return jax.shard_map(
        shards,
        mesh=mesh,
        in_specs=(
            P("dp", "mp"),
            P("dp", "mp"),
            P("dp", None),
            P("dp", None),
            P("dp", None, "mp"),
            P("dp", None, "mp"),
            P("dp", None, None, "mp"),
            P("dp", None),
            P("dp", None),
            P("dp", None),
            P("dp"),
            P("dp", None, "mp"),
        ),
        out_specs=P("dp", "mp"),
        check_vma=False,
    )
```

time: 341 us -> 62.7 us (0.18)
  waiting for transfers between devices: 145 us -> 0 us
  local copies, waits for them, and re-layouts: 93.4 us -> 9.66 us
  Pallas kernels: 0 us -> 52.6 us
  starting transfers between devices: 39.4 us -> 0 us
  matrix products: 23.2 us -> 0 us
  other arithmetic: 21.4 us -> 0 us
  blocking collectives: 14.9 us -> 0 us
    all_to_all x5 -> x0, waiting for transfers between devices: 145 us -> none  [the longest x1 94.7 us: shards(): lax.all_to_all(selected_down_panel, 'dp', split_axis=0, concat_axis=0, ti...]
    pallas_call x0 -> x1, Pallas kernels: none -> 52.6 us  [shards(): pl.pallas_call(kernel, out_shape=jax.ShapeDtypeStruct((N, width), BF), in...]
    another operation x5 -> x0, local copies, waits for them, and re-layouts: 42.8 us -> none  [the longest x2 21.4 us: shards(): cache[:, :, 1].reshape(rows_here, MAXP * page_len, kv_heads, HD)]
    all_to_all x5 -> x0, starting transfers between devices: 39.4 us -> none  [the longest x1 11.1 us: shards(): lax.all_to_all(selected_up_panel, 'dp', split_axis=0, concat_axis=0, tile...]
    gather x5 -> x0, local copies, waits for them, and re-layouts: 35.1 us -> none  [the longest x1 15.4 us: shards(): cache = extended[request_page_table]]
    concatenate x1 -> x0, other arithmetic: 19.9 us -> none  [shards(): extended = jnp.concatenate([key_value_page_cache, arrived], 0)]
    dot_general x3 -> x0, matrix products: 17.2 us -> none  [the longest x1 7.38 us: shards(): jnp.einsum('rd,pkd->rpk', hidden, got_down, preferred_element_type=jnp.fl...]
    psum x1 -> x0, blocking collectives: 14.9 us -> none  [shards(): reduced = lax.psum(partial_rank, 'mp').astype(jnp.bfloat16)]
  transfers between devices with their start and end apart: 5 -> 0, of which waited for: 3 -> 0; matrix products, arithmetic and copies ran while one was open for 36% -> 0% of each run, Pallas kernels for 0% -> 0%
where the time goes in v1:
time: 62.7 us; the launch traced here: 62.3 us
  Pallas kernels  52.6 us (84%)
  local copies, waits for them, and re-layouts  9.66 us (15%)
    pallas_call x1, Pallas kernels, shards(): pl.pallas_call(kernel, out_shape=jax.ShapeDtypeStruct((N, width), BF), in...  52.6 us
    unnamed x21, local copies, waits for them, and re-layouts  8.89 us

profile of v1, /device:TPU:1, one launch (start us, length us, event | category | flops | bytes accessed | tf_op | source)
XLA Modules:
  0.0 62.3 jit_solution(5481849452509572218)
XLA Ops:
  0.0 0.8 %reshape.13.fresh_ref = bf16[64,256]{1,0:T(8,128)(2,1)S(1)} reshape(bf16[32,2,256]{2,1,0:T(2,128)(2,1)} %param.23) | data formatting | bytes 65536 | tf_op jit(solution)/shard_map/reshape | solution.py:480
  0.8 0.0 copy-start
  0.8 1.2 %copy-done = bf16[4,64,2048]{2,1,0:T(8,128)(2,1)S(1)} copy-done((bf16[4,64,2048]{2,1,0:T(8,128)(2,1)S(1)}, bf16[4,64,2048]{2,1,0:T(8,128)(2,1)}, u32[]{:S(2)}) %copy-start) | copy-done | bytes 1048600
  2.0 0.0 copy-start.1
  2.0 1.2 %copy-done.1 = bf16[4,64,2048]{2,1,0:T(8,128)(2,1)S(1)} copy-done((bf16[4,64,2048]{2,1,0:T(8,128)(2,1)S(1)}, bf16[4,64,2048]{2,1,0:T(8,128)(2,1)}, u32[]{:S(2)}) %copy-start.1) | copy-done | bytes 1048600
  3.2 0.0 copy-start.2
  3.2 0.9 %copy-done.2 = bf16[32,2048]{1,0:T(8,128)(2,1)S(1)} copy-done((bf16[32,2048]{1,0:T(8,128)(2,1)S(1)}, bf16[32,2048]{1,0:T(8,128)(2,1)}, u32[]{:S(2)}) %copy-start.2) | copy-done | bytes 131096
  4.1 0.0 copy-start.3
  4.1 0.9 %copy-done.3 = bf16[32,2048]{1,0:T(8,128)(2,1)S(1)} copy-done((bf16[32,2048]{1,0:T(8,128)(2,1)S(1)}, bf16[32,2048]{1,0:T(8,128)(2,1)}, u32[]{:S(2)}) %copy-start.3) | copy-done | bytes 131096
  5.0 0.0 copy-start.4
  5.0 0.7 %copy-done.4 = s32[32,4]{0,1:T(4,128)S(1)} copy-done((s32[32,4]{0,1:T(4,128)S(1)}, s32[32,4]{0,1:T(4,128)}, u32[]{:S(2)}) %copy-start.4) | copy-done | bytes 536
  5.7 0.0 copy-start.5
  5.7 0.7 %copy-done.5 = s32[32,4]{0,1:T(4,128)S(1)} copy-done((s32[32,4]{0,1:T(4,128)S(1)}, s32[32,4]{0,1:T(4,128)}, u32[]{:S(2)}) %copy-start.5) | copy-done | bytes 536
  6.4 0.0 copy-start.6
  6.4 0.7 %copy-done.6 = s32[32,1]{0,1:T(1,128)S(1)} copy-done((s32[32,1]{0,1:T(1,128)S(1)}, s32[32,1]{0,1:T(1,128)}, u32[]{:S(2)}) %copy-start.6) | copy-done | bytes 152
  7.1 0.0 copy-start.7
  7.1 0.7 %copy-done.7 = s32[1,32]{1,0:T(1,128)S(1)} copy-done((s32[1,32]{1,0:T(1,128)S(1)}, s32[1,32]{1,0:T(1,128)}, u32[]{:S(2)}) %copy-start.7) | copy-done | bytes 152
  7.7 0.0 copy-start.8
  7.7 0.7 %copy-done.8 = s32[1,32]{1,0:T(1,128)S(1)} copy-done((s32[1,32]{1,0:T(1,128)S(1)}, s32[1,32]{1,0:T(1,128)}, u32[]{:S(2)}) %copy-start.8) | copy-done | bytes 152
  8.4 0.0 copy-start.9
  8.4 0.7 %copy-done.9 = s32[32]{0:T(128)S(1)} copy-done((s32[32]{0:T(128)S(1)}, s32[32]{0:T(128)}, u32[]{:S(2)}) %copy-start.9) | copy-done | bytes 152
  9.0 52.6 %shard_map.118 = bf16[32,2048]{1,0:T(8,128)(2,1)S(1)} custom-call(s32[1,32]{1,0:T(1,128)S(1)} %bitcast.11, s32[1,32]{1,0:T(1,128)S(1)} %copy-done.7, s32[4,32]{1,0:T(4,128)S(1)} %bitcast.8, s32[1,32]{1,0:T(1,128)S(1)} %copy-done.8, s32[4,32]{1,0:T(4,128)S(1)} %bitcast.10, s32[1,32]{1,0:T(1,128)S(1)} %bitcast.12, bf16[64,256]{1,0:T(8,128)(2,1)S(1)} %reshape.13.fresh_ref, ...), custom_call_target="tpu_custom_call" | custom-call | tf_op jit(solution)/shard_map/pallas_call | solution.py:423
  61.7 0.7 %copy.14 = bf16[32,2048]{1,0:T(8,128)(2,1)} copy(bf16[32,2048]{1,0:T(8,128)(2,1)S(1)} %shard_map.118) | data formatting | bytes 262144
Async XLA Ops:
  0.8 1.2 %copy-start = (bf16[4,64,2048]{2,1,0:T(8,128)(2,1)S(1)}, bf16[4,64,2048]{2,1,0:T(8,128)(2,1)}, u32[]{:S(2)}) copy-start(bf16[4,64,2048]{2,1,0:T(8,128)(2,1)} %param.16) | copy-start | bytes 3145732
  2.0 1.2 %copy-start.1 = (bf16[4,64,2048]{2,1,0:T(8,128)(2,1)S(1)}, bf16[4,64,2048]{2,1,0:T(8,128)(2,1)}, u32[]{:S(2)}) copy-start(bf16[4,64,2048]{2,1,0:T(8,128)(2,1)} %param.17) | copy-start | bytes 3145732
  3.2 0.9 %copy-start.2 = (bf16[32,2048]{1,0:T(8,128)(2,1)S(1)}, bf16[32,2048]{1,0:T(8,128)(2,1)}, u32[]{:S(2)}) copy-start(bf16[32,2048]{1,0:T(8,128)(2,1)} %hid_hbm.1) | copy-start | bytes 393220
  4.1 0.9 %copy-start.3 = (bf16[32,2048]{1,0:T(8,128)(2,1)S(1)}, bf16[32,2048]{1,0:T(8,128)(2,1)}, u32[]{:S(2)}) copy-start(bf16[32,2048]{1,0:T(8,128)(2,1)} %base_hbm.1) | copy-start | bytes 393220
  5.0 0.7 %copy-start.4 = (s32[32,4]{0,1:T(4,128)S(1)}, s32[32,4]{0,1:T(4,128)}, u32[]{:S(2)}) copy-start(s32[32,4]{0,1:T(4,128)} %param.19) | copy-start | bytes 1540
  5.7 0.7 %copy-start.5 = (s32[32,4]{0,1:T(4,128)S(1)}, s32[32,4]{0,1:T(4,128)}, u32[]{:S(2)}) copy-start(s32[32,4]{0,1:T(4,128)} %param.21) | copy-start | bytes 1540
  6.4 0.7 %copy-start.6 = (s32[32,1]{0,1:T(1,128)S(1)}, s32[32,1]{0,1:T(1,128)}, u32[]{:S(2)}) copy-start(s32[32,1]{0,1:T(1,128)} %param.14) | copy-start | bytes 388
  7.1 0.7 %copy-start.7 = (s32[1,32]{1,0:T(1,128)S(1)}, s32[1,32]{1,0:T(1,128)}, u32[]{:S(2)}) copy-start(s32[1,32]{1,0:T(1,128)} %fetch_ref.1) | copy-start | bytes 388
  7.7 0.7 %copy-start.8 = (s32[1,32]{1,0:T(1,128)S(1)}, s32[1,32]{1,0:T(1,128)}, u32[]{:S(2)}) copy-start(s32[1,32]{1,0:T(1,128)} %move_ref.1) | copy-start | bytes 388
  8.4 0.7 %copy-start.9 = (s32[32]{0:T(128)S(1)}, s32[32]{0:T(128)}, u32[]{:S(2)}) copy-start(s32[32]{0:T(128)} %param.22) | copy-start | bytes 388

commit v2 on v1

v2 whole, which is shorter than its diff:
```python
import functools
import math

import jax
import jax.numpy as jnp
from jax import lax
from jax.experimental import pallas as pl
from jax.experimental.pallas import tpu as pltpu
from jax.sharding import PartitionSpec as P

MESH = pl.DeviceIdType.MESH
BF, F32, I32 = jnp.bfloat16, jnp.float32, jnp.int32

N = 32
Z = 4
HD = 128
HEADS = 16
PAGE = 128
MAXP = 4
RANK = 64
CH = 8
CW = 256
ROWS = N * HEADS
SCALE = 1.0 / math.sqrt(HD)
LOW = -1e30
NT = (((1,), (1,)), ((), ()))


def iota(shape, dim):
    return lax.broadcasted_iota(I32, shape, dim)


def hot(mask):
    return jnp.where(mask, 1.0, 0.0).astype(BF)


def dot(a, b):
    return jnp.dot(a, b, preferred_element_type=F32)


def pieces(x):
    hi = x.astype(BF).astype(F32)
    mid = (x - hi).astype(BF).astype(F32)
    return hi, mid, x - hi - mid


def block_select(left, right, rows):
    low_heads = (iota((rows, 1), 0) & 8) == 0
    return jnp.where(low_heads, left, right)


def kernel(
    own_hbm, fetch_hbm, tab_hbm, move_hbm, mask_hbm, len_hbm, fresh_hbm,
    hid_hbm, base_hbm, down_hbm, up_hbm, cache_hbm,
    out_ref,
    own_ref, fetch_ref, tab_ref, move_ref, mask_ref, len_ref, fresh_ref, tab_s,
    hid, base, down, up, cache,
    hsend, hrecv, dsend, drecv, tsend, trecv, tsm, zbuf,
    qsend, qrecv, psend, precv, lsend, lrecv,
    pm, pinv, ph, gm, qsel, ex, cx, st1, st2,
    qbd, fkv, sl, wl, lbias, sbias, mbias, ol, loc, locp,
    lsem, ssem, rsem, gsem,
):
    d0 = lax.axis_index("dp")
    z0 = lax.axis_index("mp")
    y0 = lax.div(d0, 8)
    x0 = lax.rem(d0, 8)

    barrier = pltpu.get_barrier_semaphore()

    def peers(dy, visit):
        row = lax.rem(y0 + dy, 4) * 8

        def body(k, _):
            visit(row + lax.rem(x0 + 4 + k + (lax.div(k, 4) if dy == 0 else 0), 8))
            return 0

        lax.fori_loop(0, 7 if dy == 0 else 8, body, 0)

    def greet(t):
        pl.semaphore_signal(barrier, inc=1, device_id={"dp": t}, device_id_type=MESH)

    for dy in (2, 1, 3, 0):
        peers(dy, greet)
    for k in range(1, Z):
        pl.semaphore_signal(
            barrier, inc=1, device_id={"mp": lax.rem(z0 + k, Z)}, device_id_type=MESH
        )

    cp_hid = pltpu.make_async_copy(hid_hbm, hid, lsem.at[0])
    cp_base = pltpu.make_async_copy(base_hbm, base, lsem.at[1])
    cp_down = pltpu.make_async_copy(down_hbm, down, lsem.at[2])
    cp_up = pltpu.make_async_copy(up_hbm, up, lsem.at[3])
    cp_cache = pltpu.make_async_copy(cache_hbm, cache, lsem.at[4])
    small = [
        pltpu.make_async_copy(src, dst, lsem.at[6 + i])
        for i, (src, dst) in enumerate((
            (own_hbm, own_ref), (fetch_hbm, fetch_ref), (tab_hbm, tab_ref),
            (move_hbm, move_ref), (mask_hbm, mask_ref), (len_hbm, len_ref),
            (fresh_hbm, fresh_ref), (tab_hbm, tab_s),
        ))
    ]
    for cp in (*small, cp_hid, cp_down, cp_up, cp_base, cp_cache):
        cp.start()

    def sender(src, dst, rows, send_sem, recv_sem):
        def visit(t):
            pltpu.make_async_remote_copy(
                src_ref=src.at[pl.ds(pl.multiple_of(t * rows, rows), rows)],
                dst_ref=dst.at[pl.ds(pl.multiple_of(d0 * rows, rows), rows)],
                send_sem=send_sem,
                recv_sem=recv_sem,
                device_id={"dp": t},
                device_id_type=MESH,
            ).start()

        return visit

    def scatter(src, dst, rows, which):
        for dy in (2, 1, 3, 0):
            peers(dy, sender(src, dst, rows, ssem.at[which], rsem.at[which]))

    def drain(ref, rows, sem, count=N - 1):
        part = ref.at[pl.ds(0, count * rows)]
        pltpu.make_async_copy(part, part, sem).wait()

    def keep(src, dst, rows):
        here = pl.ds(pl.multiple_of(d0 * rows, rows), rows)
        dst[here, :] = src[here, :]

    ri, ci = iota((N, N), 0), iota((N, N), 1)
    rif, cif = ri.astype(F32), ci.astype(F32)

    def column(row):
        return jnp.sum(jnp.where(ri == ci, row, 0.0), axis=1, keepdims=True)

    for cp in small[:6]:
        cp.wait()
    own_r = own_ref[...].astype(F32)
    own_c = column(own_r)
    same = own_c == own_r
    rank_c = jnp.sum(jnp.where(same & (ci < ri), 1.0, 0.0), axis=1, keepdims=True)
    key_c = own_c * HEADS + rank_c * CH
    length = len_ref[...].astype(F32)
    fetch_c = column(fetch_ref[...].astype(F32))
    move_c = column(move_ref[...].astype(F32))
    req_c = jnp.zeros((N, 1), F32)
    nlp_c = jnp.zeros((N, 1), F32)
    remote = jnp.zeros((N, N), F32)
    local_live = []
    for j in range(MAXP):
        tab_r = tab_ref[j : j + 1, :].astype(F32)
        live_r = jnp.where(
            mask_ref[j : j + 1, :] == 1, jnp.clip(length - PAGE * j, 0.0, PAGE), 0.0
        )
        hit = tab_r == rif + PAGE
        req_c += jnp.sum(jnp.where(hit, cif + 1.0, 0.0), axis=1, keepdims=True)
        nlp_c += jnp.sum(jnp.where(hit, live_r, 0.0), axis=1, keepdims=True)
        local_live.append(column(jnp.where(tab_r < PAGE, live_r, 0.0)))
        remote += jnp.where(column(tab_r) == cif + PAGE, 1.0, 0.0)

    lane = iota((N, 128), 1)
    tsend[...] = jnp.where(
        lane == 0, fetch_c, jnp.where(lane == 1, move_c, jnp.where(lane == 2, nlp_c, 0.0))
    ).astype(I32)

    jj, rr = iota((N, CW), 1), iota((N, CW), 0)
    target = jnp.sum(
        jnp.where(rr == (jj & (N - 1)), key_c, 0.0), axis=0, keepdims=True
    ) + (jj[:1] >> 5).astype(F32)
    place = hot(iota((ROWS, CW), 0).astype(F32) == target)
    cp_hid.wait()
    chunks = jnp.concatenate([hid[:, c * CW : (c + 1) * CW] for c in range(CH)], axis=0)
    hsend[...] = dot(place, chunks).astype(BF)

    pl.semaphore_wait(barrier, N - 1 + Z - 1)
    scatter(tsend, trecv, 1, 1)
    scatter(hsend, hrecv, HEADS, 0)
    keep(tsend, trecv, 1)
    keep(hsend, hrecv, HEADS)

    blk = 128

    def rows_of(b):
        return pl.ds(pl.multiple_of(b * blk, blk), blk)

    vals = jnp.where(lane == 0, req_c, 0.0)
    for j in range(MAXP):
        vals = jnp.where(lane == j + 1, local_live[j], vals)
    vals = vals.astype(BF)
    wide = jnp.concatenate([remote] * 4, axis=1)
    for h in range(4):
        mine = (iota((N, 128), 1) >> 5) == h
        mbias[h * N : (h + 1) * N, :] = jnp.where(mine & (wide > 0.0), 0.0, LOW)
    for c in range(CH):
        gm[c * N : (c + 1) * N, :] = hot(iota((N, ROWS), 1).astype(F32) == key_c + float(c))

    def build(b, _):
        i = iota((blk, 1), 0) + b * blk
        j = iota((blk, ROWS), 1)
        at = rows_of(b)
        pm[at, :] = hot(j == ((i & 31) << 4) + (((i >> 5) & 1) << 3) + (i >> 6))
        pinv[at, :] = hot(j == ((i & 7) << 6) + (((i >> 3) & 1) << 5) + (i >> 4))
        e = hot(iota((blk, N), 1) == (i >> 4))
        ex[at, :] = e
        cx[at, :] = dot(e, vals)
        return 0

    lax.fori_loop(0, ROWS // blk, build, 0)

    cp_down.wait()
    drain(trecv, 1, rsem.at[1])
    cp_tsm = pltpu.make_async_copy(trecv, tsm, lsem.at[5])
    cp_tsm.start()
    adapter = trecv[:, 0:1].astype(F32)
    adapter = jnp.concatenate([adapter, adapter], axis=0)
    wanted = (iota((2 * N, CW), 1) >> 6).astype(F32) == adapter
    drain(hrecv, HEADS, rsem.at[0])
    arranged = dot(pm[...], hrecv[...]).astype(BF)
    acc = jnp.zeros((2 * N, CW), F32)
    for c in range(CH):
        acc += lax.dot_general(
            arranged[c * 2 * N : (c + 1) * 2 * N],
            down[:, c * CW : (c + 1) * CW],
            NT,
            preferred_element_type=F32,
        )
    acc = jnp.where(wanted, acc, 0.0)
    zbuf[pl.ds(z0, 1)] = (acc[:, :128] + acc[:, 128:])[None]
    for k in (2, 1, 3):
        pltpu.make_async_remote_copy(
            src_ref=zbuf.at[z0],
            dst_ref=zbuf.at[z0],
            send_sem=ssem.at[2],
            recv_sem=rsem.at[2],
            device_id={"mp": lax.rem(z0 + k, Z)},
            device_id_type=MESH,
        ).start()
    zpart = zbuf.at[pl.ds(0, Z - 1)]

    small[6].wait()
    fresh = fresh_ref[...].reshape(2 * N, CW)

    def build_more(b, _):
        i = iota((blk, 1), 0) + b * blk
        j = iota((blk, ROWS), 1)
        at = rows_of(b)
        head = ((i & 1) << 8) + (((i >> 1) & 7) << 5)
        req = cx[at, 0:1]
        qsel[at, :] = hot(
            j.astype(F32) == jnp.where(req > 0.0, req - 1.0 + head.astype(F32), -1.0)
        )
        qsel[pl.ds(pl.multiple_of(ROWS + b * blk, blk), blk), :] = hot(j == head + (i >> 4))
        return 0

    lax.fori_loop(0, ROWS // blk, build_more, 0)
    cp_up.wait()
    pltpu.make_async_copy(zpart, zpart, rsem.at[2]).wait()
    u = (zbuf[0] + zbuf[1]) + (zbuf[2] + zbuf[3])
    u = jnp.where(wanted, jnp.concatenate([u, u], axis=1), 0.0).astype(BF)
    for c in range(CH):
        st1[c * 2 * N : (c + 1) * 2 * N, :] = dot(u, up[:, c * CW : (c + 1) * CW]).astype(BF)
    for dy in (2, 1, 3, 0):
        at = pl.ds(pl.multiple_of(lax.rem(y0 + dy, 4) * 128, 128), 128)
        dsend[at, :] = dot(pinv[at, :], st1[...]).astype(BF)
        peers(dy, sender(dsend, drecv, HEADS, ssem.at[3], rsem.at[3]))
    keep(dsend, drecv, HEADS)

    counts = trecv[...].astype(F32).astype(BF)

    def build_masks(b, _):
        i = iota((blk, 1), 0) + b * blk
        j = iota((blk, ROWS), 1)
        t = iota((blk, PAGE), 1).astype(F32)
        at = rows_of(b)
        ph[at, :] = hot(j == ((i & 31) << 4) + (i >> 5))
        n_live = dot(ex[at, :], counts)[:, 2:3]
        sbias[at, :] = jnp.where(t < n_live, 0.0, LOW)
        x = cx[at, :]
        for k in range(MAXP):
            lbias[at, k * PAGE : (k + 1) * PAGE] = jnp.where(t < x[:, k + 1 : k + 2], 0.0, LOW)
        k0 = dot(hot(iota((blk, 2 * N), 1) == (i >> 4) * 2), fresh)
        v0 = dot(hot(iota((blk, 2 * N), 1) == (i >> 4) * 2 + 1), fresh)
        fkv[at, :] = jnp.concatenate(
            [
                block_select(k0[:, :HD], k0[:, HD:], blk),
                block_select(v0[:, :HD], v0[:, HD:], blk),
            ],
            axis=1,
        )
        return 0

    lax.fori_loop(0, ROWS // blk, build_masks, 0)
    cp_base.wait()
    base_re = jnp.concatenate([base[:, c * CW : (c + 1) * CW] for c in range(CH)], axis=0)
    base_re = base_re.astype(F32)
    halves = iota((128, CW), 1) >> 7
    heads_of = hot(halves == ((iota((128, CW), 0) >> 3) & 1))

    drain(drecv, HEADS, rsem.at[3])
    query = (base_re + 2.0 * dot(gm[...], drecv[...])).astype(BF)
    st2[:CW, :] = query[:, :HD]
    st2[CW:, :] = query[:, HD:]
    for dy in (2, 1, 3, 0):
        at = pl.ds(pl.multiple_of(lax.rem(y0 + dy, 4) * 128, 128), 128)
        qsend[at, :] = dot(qsel[at, :], st2[...]).astype(BF)
        peers(dy, sender(qsend, qrecv, HEADS, ssem.at[4], gsem.at[dy]))
    keep(qsend, qrecv, HEADS)

    def spread_heads(q):
        return jnp.concatenate([q, q], axis=1) * heads_of

    for b in range(ROWS // 128):
        at = slice(b * 128, (b + 1) * 128)
        mine = dot(qsel[ROWS + b * 128 : ROWS + (b + 1) * 128, :], st2[...])
        qbd[at, :] = spread_heads(mine.astype(BF))
        loc[at, 0:1] = jnp.sum(mine * fkv[at, :HD], axis=1, keepdims=True) * SCALE

    cp_cache.wait()
    small[7].wait()

    def local_scores(r, _):
        at = pl.ds(pl.multiple_of(r * HEADS, HEADS), HEADS)
        q = qbd[at, :]
        for j in range(MAXP):
            page = jnp.minimum(tab_s[j, r], PAGE - 1)
            sl[at, j * PAGE : (j + 1) * PAGE] = lax.dot_general(
                q, cache[page, 0], NT, preferred_element_type=F32
            )
        return 0

    lax.fori_loop(0, N, local_scores, 0, unroll=8)

    cp_tsm.wait()
    for dy in (0, 1, 3, 2):
        row = lax.rem(y0 + 4 - dy, 4)
        at = pl.ds(pl.multiple_of(row * 128, 128), 128)
        drain(qrecv, HEADS, gsem.at[dy], 7 if dy == 0 else 8)
        q = spread_heads(qrecv[at, :])
        pages = [jnp.clip(tsm[row * 8 + i, 1], 0, PAGE - 1) for i in range(8)]
        s = jnp.concatenate(
            [
                lax.dot_general(
                    q[i * HEADS : (i + 1) * HEADS],
                    cache[pages[i], 0],
                    NT,
                    preferred_element_type=F32,
                )
                for i in range(8)
            ],
            axis=0,
        )
        s = s * SCALE + sbias[at, :]
        m = jnp.max(s, axis=1, keepdims=True)
        w = jnp.exp(s - m)
        total = jnp.sum(w, axis=1, keepdims=True)
        w = w.astype(BF)
        o = jnp.concatenate(
            [dot(w[i * HEADS : (i + 1) * HEADS], cache[pages[i], 1]) for i in range(8)], axis=0
        )
        psend[at, :] = (block_select(o[:, :HD], o[:, HD:], 128) / total).astype(BF)
        lse = jnp.where(
            iota((128, 128), 1) == (iota((128, 128), 0) & 15), m + jnp.log(total), 0.0
        )
        lsend[pl.ds(pl.multiple_of(row * 8, 8), 8), :] = jnp.sum(
            lse.reshape(8, HEADS, 128), axis=1
        )
        back = (4 - dy) % 4
        peers(back, sender(lsend, lrecv, 1, ssem.at[6], rsem.at[6]))
        peers(back, sender(psend, precv, HEADS, ssem.at[5], rsem.at[5]))
    keep(lsend, lrecv, 1)
    keep(psend, precv, HEADS)

    def local_weights(b, _):
        at = rows_of(b)
        new = loc[at, 0:1]
        parts = [
            sl[at, j * PAGE : (j + 1) * PAGE] * SCALE + lbias[at, j * PAGE : (j + 1) * PAGE]
            for j in range(MAXP)
        ]
        m = jnp.maximum(jnp.maximum(parts[0], parts[1]), jnp.maximum(parts[2], parts[3]))
        m = jnp.maximum(jnp.max(m, axis=1, keepdims=True), new)
        wf = jnp.exp(new - m)
        total = jnp.zeros((blk, PAGE), F32)
        for j in range(MAXP):
            w = jnp.exp(parts[j] - m)
            total += w
            wl[at, j * PAGE : (j + 1) * PAGE] = w.astype(BF)
        total = jnp.sum(total, axis=1, keepdims=True) + wf
        at_lane = iota((blk, 128), 1)
        stat = jnp.where(at_lane == 0, m, jnp.where(at_lane == 1, total, 0.0))
        loc[at, :] = jnp.where(at_lane == 2, wf, stat)
        return 0

    lax.fori_loop(0, ROWS // blk, local_weights, 0)

    def local_values(r, _):
        at = pl.ds(pl.multiple_of(r * HEADS, HEADS), HEADS)
        o = jnp.zeros((HEADS, CW), F32)
        for j in range(MAXP):
            page = jnp.minimum(tab_s[j, r], PAGE - 1)
            o += dot(wl[at, j * PAGE : (j + 1) * PAGE], cache[page, 1])
        ol[at, :] = block_select(o[:, :HD], o[:, HD:], HEADS)
        return 0

    lax.fori_loop(0, N, local_values, 0, unroll=8)

    def local_part(b, _):
        at = rows_of(b)
        st = loc[at, :]
        m, total, wf = st[:, 0:1], st[:, 1:2], st[:, 2:3].astype(BF).astype(F32)
        o = (ol[at, :] + wf * fkv[at, HD:]) / total
        hi, mid, lo = pieces(m + jnp.log(total))
        at_lane = iota((blk, 128), 1)
        stat = jnp.where(at_lane == 0, hi, jnp.where(at_lane == 1, mid, 0.0))
        stat = jnp.where(at_lane == 2, lo, stat)
        locp[at, :HD] = o.astype(BF)
        locp[at, HD:] = stat.astype(BF)
        return 0

    lax.fori_loop(0, ROWS // blk, local_part, 0)
    mine = dot(ph[...], locp[...])
    ol[...] = mine[:, :HD]
    loc[...] = jnp.broadcast_to(
        mine[:, HD : HD + 1] + mine[:, HD + 1 : HD + 2] + mine[:, HD + 2 : HD + 3], (ROWS, 128)
    )

    drain(lrecv, 1, rsem.at[6])
    stats = jnp.transpose(lrecv[...])
    drain(precv, HEADS, rsem.at[5])
    others = dot(ph[...], precv[...]).astype(BF)
    others = jnp.concatenate([others, jnp.ones((ROWS, 128), BF)], axis=1)
    for g in range(4):
        at = slice(g * 128, (g + 1) * 128)
        row = jnp.concatenate([stats[4 * g + i : 4 * g + i + 1, :] for i in range(4)], axis=1)
        lse = row + mbias[...]
        mine = loc[at, :]
        top = jnp.maximum(jnp.max(lse, axis=1, keepdims=True), mine)
        both = dot(jnp.exp(lse - top).astype(BF), others[at])
        wm = jnp.exp(mine - top)
        o = (both[:, :HD] + wm * ol[at, :]) / (both[:, HD:] + wm)
        for i in range(4):
            h = 4 * g + i
            out_ref[:, h * HD : (h + 1) * HD] = o[i * N : (i + 1) * N].astype(BF)

    drain(hsend, HEADS, ssem.at[0])
    drain(tsend, 1, ssem.at[1])
    pltpu.make_async_copy(zpart, zpart, ssem.at[2]).wait()
    drain(dsend, HEADS, ssem.at[3])
    drain(qsend, HEADS, ssem.at[4])
    drain(psend, HEADS, ssem.at[5])
    drain(lsend, 1, ssem.at[6])


def shards(
    hidden,
    base_query_projection,
    adapter_owner_map,
    adapter_fetch_table,
    adapter_down_panels,
    adapter_up_panels,
    key_value_page_cache,
    request_page_table,
    page_transfer_table,
    page_entry_mask,
    lengths,
    fresh_key_value,
):
    width = N * 64
    table = request_page_table.T
    vmem = pl.BlockSpec(memory_space=pltpu.VMEM)
    hbm = pl.BlockSpec(memory_space=pltpu.HBM)
    v = pltpu.VMEM
    return pl.pallas_call(
        kernel,
        out_shape=jax.ShapeDtypeStruct((N, width), BF),
        in_specs=[hbm] * 12,
        out_specs=vmem,
        scratch_shapes=[
            v((1, N), I32),
            v((1, N), I32),
            v((MAXP, N), I32),
            v((1, N), I32),
            v((MAXP, N), I32),
            v((1, N), I32),
            v((N, 2, CW), BF),
            pltpu.SMEM((MAXP, N), I32),
            v((N, width), BF),
            v((N, width), BF),
            v((CW, width), BF),
            v((CW, width), BF),
            v((PAGE, 2, PAGE, CW), BF),
            v((ROWS, CW), BF),
            v((ROWS, CW), BF),
            v((ROWS, CW), BF),
            v((ROWS, CW), BF),
            v((N, 128), I32),
            v((N, 128), I32),
            pltpu.SMEM((N, 128), I32),
            v((Z, 2 * N, 128), F32),
            v((ROWS, HD), BF),
            v((ROWS, HD), BF),
            v((ROWS, HD), BF),
            v((ROWS, HD), BF),
            v((N, 128), F32),
            v((N, 128), F32),
            v((ROWS, ROWS), BF),
            v((ROWS, ROWS), BF),
            v((ROWS, ROWS), BF),
            v((CW, ROWS), BF),
            v((2 * ROWS, ROWS), BF),
            v((ROWS, N), BF),
            v((ROWS, 128), F32),
            v((ROWS, CW), BF),
            v((ROWS, HD), BF),
            v((ROWS, CW), BF),
            v((ROWS, CW), F32),
            v((ROWS, ROWS), F32),
            v((ROWS, ROWS), BF),
            v((ROWS, ROWS), F32),
            v((ROWS, PAGE), F32),
            v((128, 128), F32),
            v((ROWS, HD), F32),
            v((ROWS, 128), F32),
            v((ROWS, CW), BF),
            pltpu.SemaphoreType.DMA((14,)),
            pltpu.SemaphoreType.DMA((7,)),
            pltpu.SemaphoreType.DMA((7,)),
            pltpu.SemaphoreType.DMA((4,)),
        ],
        compiler_params=pltpu.CompilerParams(
            collective_id=0, has_side_effects=True, vmem_limit_bytes=63 * 1024 * 1024
        ),
    )(
        adapter_owner_map.T,
        adapter_fetch_table,
        table,
        page_transfer_table,
        page_entry_mask.T,
        lengths.reshape(1, N),
        fresh_key_value,
        hidden,
        base_query_projection,
        adapter_down_panels.reshape(CW, width),
        adapter_up_panels.reshape(CW, width),
        key_value_page_cache,
    )


def solution(mesh):
    return jax.shard_map(
        shards,
        mesh=mesh,
        in_specs=(
            P("dp", "mp"),
            P("dp", "mp"),
            P("dp", None),
            P("dp", None),
            P("dp", None, "mp"),
            P("dp", None, "mp"),
            P("dp", None, None, "mp"),
            P("dp", None),
            P("dp", None),
            P("dp", None),
            P("dp"),
            P("dp", None, "mp"),
        ),
        out_specs=P("dp", "mp"),
        check_vma=False,
    )
```

time: 62.7 us -> 41.4 us (0.66)
  Pallas kernels: 52.6 us -> 39.7 us
  local copies, waits for them, and re-layouts: 9.66 us -> 1.57 us
    pallas_call x1, Pallas kernels: 52.6 us -> 39.7 us  [shards(): pl.pallas_call(kernel, out_shape=jax.ShapeDtypeStruct((N, width), BF), in...]
    unnamed x21 -> x1, local copies, waits for them, and re-layouts: 8.89 us -> 1.57 us
    reshape x1 -> x0, local copies, waits for them, and re-layouts: 0.77 us -> none  [shards(): fresh_key_value.reshape(2 * N, CW)]
where the time goes in v2:
time: 41.4 us; the launch traced here: 41.3 us
  Pallas kernels  39.7 us (96%)
  local copies, waits for them, and re-layouts  1.57 us (4%)
    pallas_call x1, Pallas kernels, shards(): pl.pallas_call(kernel, out_shape=jax.ShapeDtypeStruct((N, width), BF), in...  39.7 us
    unnamed x1, local copies, waits for them, and re-layouts  1.57 us

profile of v2, /device:TPU:1, one launch (start us, length us, event | category | flops | bytes accessed | tf_op | source)
XLA Modules:
  0.0 41.3 jit_solution(1091547008475327416)
XLA Ops:
  0.0 39.7 %shard_map.118 = bf16[32,2048]{1,0:T(8,128)(2,1)} custom-call(s32[1,32]{1,0:T(1,128)} %bitcast.10, s32[1,32]{1,0:T(1,128)} %fetch_hbm.1, s32[4,32]{1,0:T(4,128)} %bitcast.8, s32[1,32]{1,0:T(1,128)} %move_hbm.1, s32[4,32]{1,0:T(4,128)} %bitcast.9, s32[1,32]{1,0:T(1,128)} %bitcast.11, bf16[32,2,256]{2,1,0:T(2,128)(2,1)} %fresh_hbm.1, ...), custom_call_target="tpu_custom_call" | custom-call | tf_op jit(solution)/shard_map/pallas_call | solution.py:474
  39.7 1.6 %copy.14 = bf16[32,2048]{1,0:T(8,128)(2,1)} copy(bf16[32,2048]{1,0:T(8,128)(2,1)} %shard_map.118) | data formatting | bytes 262144

commit v3 on v2

--- a/solution.py
+++ b/solution.py
@@ -21,6 +21,7 @@
 CH = 8
 CW = 256
 ROWS = N * HEADS
+FAR = (0, 1, 2, 1)
 SCALE = 1.0 / math.sqrt(HD)
 LOW = -1e30
 NT = (((1,), (1,)), ((), ()))
@@ -54,30 +55,28 @@
     hid_hbm, base_hbm, down_hbm, up_hbm, cache_hbm,
     out_ref,
     own_ref, fetch_ref, tab_ref, move_ref, mask_ref, len_ref, fresh_ref, tab_s,
-    hid, base, down, up, cache,
+    hid, base, down, up, cache, kt, kts,
     hsend, hrecv, dsend, drecv, tsend, trecv, tsm, zbuf,
     qsend, qrecv, psend, precv, lsend, lrecv,
-    pm, pinv, ph, gm, qsel, ex, cx, st1, st2,
+    turn, ph, qsel, ex, cx, st1, basep, basel,
     qbd, fkv, sl, wl, lbias, sbias, mbias, ol, loc, locp,
     lsem, ssem, rsem, gsem,
 ):
     d0 = lax.axis_index("dp")
     z0 = lax.axis_index("mp")
-    y0 = lax.div(d0, 8)
-    x0 = lax.rem(d0, 8)
+    y0, x0, c0 = lax.div(d0, 8), lax.rem(lax.div(d0, 2), 4), lax.rem(d0, 2)
+    rows8 = [lax.rem(y0 + dy, 4) * 8 for dy in range(4)]
+    around = [[lax.rem(x0 + dx, 4) * 2 + c for c in (c0, 1 - c0)] for dx in range(4)]
 
     barrier = pltpu.get_barrier_semaphore()
 
     def peers(dy, visit):
-        row = lax.rem(y0 + dy, 4) * 8
-
-        def body(k, _):
-            visit(row + lax.rem(x0 + 4 + k + (lax.div(k, 4) if dy == 0 else 0), 8))
-            return 0
-
-        lax.fori_loop(0, 7 if dy == 0 else 8, body, 0)
-
-    def greet(t):
+        for dx in (2, 1, 3, 0):
+            for dc in (1, 0):
+                if (dy, dx, dc) != (0, 0, 0):
+                    visit(rows8[dy] + around[dx][dc], FAR[dy] + FAR[dx])
+
+    def greet(t, _):
         pl.semaphore_signal(barrier, inc=1, device_id={"dp": t}, device_id_type=MESH)
 
     for dy in (2, 1, 3, 0):
@@ -103,13 +102,13 @@
     for cp in (*small, cp_hid, cp_down, cp_up, cp_base, cp_cache):
         cp.start()
 
-    def sender(src, dst, rows, send_sem, recv_sem):
-        def visit(t):
+    def sender(src, dst, rows, send_sem, recv_sem, per_hops=None):
+        def visit(t, hops):
             pltpu.make_async_remote_copy(
                 src_ref=src.at[pl.ds(pl.multiple_of(t * rows, rows), rows)],
                 dst_ref=dst.at[pl.ds(pl.multiple_of(d0 * rows, rows), rows)],
                 send_sem=send_sem,
-                recv_sem=recv_sem,
+                recv_sem=recv_sem if per_hops is None else per_hops.at[hops],
                 device_id={"dp": t},
                 device_id_type=MESH,
             ).start()
@@ -146,6 +145,8 @@
     move_c = column(move_ref[...].astype(F32))
     req_c = jnp.zeros((N, 1), F32)
     nlp_c = jnp.zeros((N, 1), F32)
+    slot_req_c = jnp.zeros((N, 1), F32)
+    key_r = jnp.sum(jnp.where(ri == ci, key_c, 0.0), axis=0, keepdims=True)
     remote = jnp.zeros((N, N), F32)
     local_live = []
     for j in range(MAXP):
@@ -155,6 +156,7 @@
         )
         hit = tab_r == rif + PAGE
         req_c += jnp.sum(jnp.where(hit, cif + 1.0, 0.0), axis=1, keepdims=True)
+        slot_req_c += jnp.sum(jnp.where(hit, key_r / CH, 0.0), axis=1, keepdims=True)
         nlp_c += jnp.sum(jnp.where(hit, live_r, 0.0), axis=1, keepdims=True)
         local_live.append(column(jnp.where(tab_r < PAGE, live_r, 0.0)))
         remote += jnp.where(column(tab_r) == cif + PAGE, 1.0, 0.0)
@@ -173,12 +175,6 @@
     chunks = jnp.concatenate([hid[:, c * CW : (c + 1) * CW] for c in range(CH)], axis=0)
     hsend[...] = dot(place, chunks).astype(BF)
 
-    pl.semaphore_wait(barrier, N - 1 + Z - 1)
-    scatter(tsend, trecv, 1, 1)
-    scatter(hsend, hrecv, HEADS, 0)
-    keep(tsend, trecv, 1)
-    keep(hsend, hrecv, HEADS)
-
     blk = 128
 
     def rows_of(b):
@@ -187,44 +183,71 @@
     vals = jnp.where(lane == 0, req_c, 0.0)
     for j in range(MAXP):
         vals = jnp.where(lane == j + 1, local_live[j], vals)
+    vals = jnp.where(lane == 5, slot_req_c, jnp.where(lane == 6, key_c / CH, vals))
     vals = vals.astype(BF)
     wide = jnp.concatenate([remote] * 4, axis=1)
     for h in range(4):
         mine = (iota((N, 128), 1) >> 5) == h
         mbias[h * N : (h + 1) * N, :] = jnp.where(mine & (wide > 0.0), 0.0, LOW)
-    for c in range(CH):
-        gm[c * N : (c + 1) * N, :] = hot(iota((N, ROWS), 1).astype(F32) == key_c + float(c))
+    i128, j128 = iota((128, 128), 0), iota((128, 128), 1)
+    turn[...] = hot(j128 == ((i128 & 7) << 4) + (((i128 >> 3) & 1) << 3) + (i128 >> 4))
 
     def build(b, _):
         i = iota((blk, 1), 0) + b * blk
         j = iota((blk, ROWS), 1)
         at = rows_of(b)
-        pm[at, :] = hot(j == ((i & 31) << 4) + (((i >> 5) & 1) << 3) + (i >> 6))
-        pinv[at, :] = hot(j == ((i & 7) << 6) + (((i >> 3) & 1) << 5) + (i >> 4))
         e = hot(iota((blk, N), 1) == (i >> 4))
         ex[at, :] = e
-        cx[at, :] = dot(e, vals)
+        x = dot(e, vals)
+        cx[at, :] = x
+        chunk = (i >> 1) & 7
+        jf = j.astype(F32)
+        wants = x[:, 5:6] * CH + chunk.astype(F32)
+        qsel[at, :] = hot(jf == jnp.where(x[:, 0:1] > 0.0, wants, -1.0))
+        mine = x[:, 6:7] * CH + chunk.astype(F32)
+        qsel[pl.ds(pl.multiple_of(ROWS + b * blk, blk), blk), :] = hot(jf == mine)
         return 0
 
     lax.fori_loop(0, ROWS // blk, build, 0)
 
+    pl.semaphore_wait(barrier, N - 1 + Z - 1)
+    scatter(hsend, hrecv, HEADS, 0)
+    scatter(tsend, trecv, 1, 1)
+    keep(tsend, trecv, 1)
+    keep(hsend, hrecv, HEADS)
+
+    cp_cache.wait()
+    small[7].wait()
+
+    def turn_local(r, _):
+        for j in range(MAXP):
+            page = jnp.minimum(tab_s[j, r], PAGE - 1)
+            kt[r, :, j * PAGE : (j + 1) * PAGE] = jnp.transpose(cache[page, 0])
+        return 0
+
+    lax.fori_loop(0, N, turn_local, 0, unroll=4)
+
     cp_down.wait()
+    drain(hrecv, HEADS, rsem.at[0])
+    arranged = [
+        dot(turn[...], hrecv[g * 128 : (g + 1) * 128, :]).astype(BF) for g in range(4)
+    ]
+    acc = jnp.zeros((2 * N, CW), F32)
+    for c in range(CH):
+        acc += lax.dot_general(
+            jnp.concatenate([x[c * 16 : (c + 1) * 16] for x in arranged], axis=0),
+            down[:, c * CW : (c + 1) * CW],
+            NT,
+            preferred_element_type=F32,
+        )
     drain(trecv, 1, rsem.at[1])
     cp_tsm = pltpu.make_async_copy(trecv, tsm, lsem.at[5])
     cp_tsm.start()
     adapter = trecv[:, 0:1].astype(F32)
-    adapter = jnp.concatenate([adapter, adapter], axis=0)
+    adapter = jnp.concatenate(
+        [adapter[g * 8 : (g + 1) * 8] for g in (0, 0, 1, 1, 2, 2, 3, 3)], axis=0
+    )
     wanted = (iota((2 * N, CW), 1) >> 6).astype(F32) == adapter
-    drain(hrecv, HEADS, rsem.at[0])
-    arranged = dot(pm[...], hrecv[...]).astype(BF)
-    acc = jnp.zeros((2 * N, CW), F32)
-    for c in range(CH):
-        acc += lax.dot_general(
-            arranged[c * 2 * N : (c + 1) * 2 * N],
-            down[:, c * CW : (c + 1) * CW],
-            NT,
-            preferred_element_type=F32,
-        )
     acc = jnp.where(wanted, acc, 0.0)
     zbuf[pl.ds(z0, 1)] = (acc[:, :128] + acc[:, 128:])[None]
     for k in (2, 1, 3):
@@ -238,34 +261,30 @@
         ).start()
     zpart = zbuf.at[pl.ds(0, Z - 1)]
 
-    small[6].wait()
-    fresh = fresh_ref[...].reshape(2 * N, CW)
-
-    def build_more(b, _):
-        i = iota((blk, 1), 0) + b * blk
-        j = iota((blk, ROWS), 1)
-        at = rows_of(b)
-        head = ((i & 1) << 8) + (((i >> 1) & 7) << 5)
-        req = cx[at, 0:1]
-        qsel[at, :] = hot(
-            j.astype(F32) == jnp.where(req > 0.0, req - 1.0 + head.astype(F32), -1.0)
-        )
-        qsel[pl.ds(pl.multiple_of(ROWS + b * blk, blk), blk), :] = hot(j == head + (i >> 4))
-        return 0
-
-    lax.fori_loop(0, ROWS // blk, build_more, 0)
+    cp_tsm.wait()
+
+    def turn_served(d, _):
+        kts[d] = jnp.transpose(cache[jnp.clip(tsm[d, 1], 0, PAGE - 1), 0])
+        return 0
+
+    lax.fori_loop(0, N, turn_served, 0, unroll=8)
     cp_up.wait()
     pltpu.make_async_copy(zpart, zpart, rsem.at[2]).wait()
     u = (zbuf[0] + zbuf[1]) + (zbuf[2] + zbuf[3])
     u = jnp.where(wanted, jnp.concatenate([u, u], axis=1), 0.0).astype(BF)
-    for c in range(CH):
-        st1[c * 2 * N : (c + 1) * 2 * N, :] = dot(u, up[:, c * CW : (c + 1) * CW]).astype(BF)
+    deltas = [dot(u, up[:, c * CW : (c + 1) * CW]).astype(BF) for c in range(CH)]
+    for g in range(4):
+        st1[g * 128 : (g + 1) * 128, :] = jnp.concatenate(
+            [x[g * 16 : (g + 1) * 16] for x in deltas], axis=0
+        )
     for dy in (2, 1, 3, 0):
-        at = pl.ds(pl.multiple_of(lax.rem(y0 + dy, 4) * 128, 128), 128)
-        dsend[at, :] = dot(pinv[at, :], st1[...]).astype(BF)
+        at = pl.ds(pl.multiple_of(rows8[dy] * 16, 128), 128)
+        dsend[at, :] = dot(turn[...], st1[at, :]).astype(BF)
         peers(dy, sender(dsend, drecv, HEADS, ssem.at[3], rsem.at[3]))
     keep(dsend, drecv, HEADS)
 
+    small[6].wait()
+    fresh = fresh_ref[...].reshape(2 * N, CW)
     counts = trecv[...].astype(F32).astype(BF)
 
     def build_masks(b, _):
@@ -292,87 +311,55 @@
 
     lax.fori_loop(0, ROWS // blk, build_masks, 0)
     cp_base.wait()
-    base_re = jnp.concatenate([base[:, c * CW : (c + 1) * CW] for c in range(CH)], axis=0)
-    base_re = base_re.astype(F32)
-    halves = iota((128, CW), 1) >> 7
-    heads_of = hot(halves == ((iota((128, CW), 0) >> 3) & 1))
+    chunked = jnp.concatenate([base[:, c * CW : (c + 1) * CW] for c in range(CH)], axis=0)
+
+    def build_base(b, _):
+        i = iota((blk, 1), 0) + b * blk
+        j = iota((blk, CW), 1)
+        at = rows_of(b)
+        head = ((i >> 1) & 7) << 5
+        req = cx[at, 0:1]
+        want = jnp.where(req > 0.0, req - 1.0 + head.astype(F32), -1.0)
+        both = dot(hot(j.astype(F32) == want), chunked)
+        basep[at, :] = jnp.where((i & 1) == 0, both[:, :HD], both[:, HD:])
+        both = dot(hot(j == head + (i >> 4)), chunked)
+        basel[at, :] = jnp.where((i & 1) == 0, both[:, :HD], both[:, HD:])
+        return 0
+
+    lax.fori_loop(0, ROWS // blk, build_base, 0)
+    odd = (iota((128, 1), 0) & 1) == 1
+    halves = iota((HEADS, CW), 1) >> 7
+    heads_of = hot(halves == ((iota((HEADS, CW), 0) >> 3) & 1))
 
     drain(drecv, HEADS, rsem.at[3])
-    query = (base_re + 2.0 * dot(gm[...], drecv[...])).astype(BF)
-    st2[:CW, :] = query[:, :HD]
-    st2[CW:, :] = query[:, HD:]
+
+    def pick(selector, base_rows):
+        both = dot(selector, drecv[...])
+        return (base_rows + 2.0 * jnp.where(odd, both[:, HD:], both[:, :HD])).astype(BF)
+
     for dy in (2, 1, 3, 0):
-        at = pl.ds(pl.multiple_of(lax.rem(y0 + dy, 4) * 128, 128), 128)
-        qsend[at, :] = dot(qsel[at, :], st2[...]).astype(BF)
-        peers(dy, sender(qsend, qrecv, HEADS, ssem.at[4], gsem.at[dy]))
+        at = pl.ds(pl.multiple_of(rows8[dy] * 16, 128), 128)
+        qsend[at, :] = pick(qsel[at, :], basep[at, :])
+        peers(dy, sender(qsend, qrecv, HEADS, ssem.at[4], None, gsem))
     keep(qsend, qrecv, HEADS)
 
     def spread_heads(q):
-        return jnp.concatenate([q, q], axis=1) * heads_of
+        return jnp.concatenate([q, q], axis=1) * jnp.concatenate([heads_of] * (q.shape[0] // HEADS), axis=0)
 
     for b in range(ROWS // 128):
         at = slice(b * 128, (b + 1) * 128)
-        mine = dot(qsel[ROWS + b * 128 : ROWS + (b + 1) * 128, :], st2[...])
-        qbd[at, :] = spread_heads(mine.astype(BF))
-        loc[at, 0:1] = jnp.sum(mine * fkv[at, :HD], axis=1, keepdims=True) * SCALE
-
-    cp_cache.wait()
-    small[7].wait()
+        mine = pick(qsel[ROWS + b * 128 : ROWS + (b + 1) * 128, :], basel[at, :])
+        qbd[at, :] = spread_heads(mine)
+        loc[at, 0:1] = jnp.sum(mine.astype(F32) * fkv[at, :HD], axis=1, keepdims=True) * SCALE
 
     def local_scores(r, _):
         at = pl.ds(pl.multiple_of(r * HEADS, HEADS), HEADS)
-        q = qbd[at, :]
-        for j in range(MAXP):
-            page = jnp.minimum(tab_s[j, r], PAGE - 1)
-            sl[at, j * PAGE : (j + 1) * PAGE] = lax.dot_general(
-                q, cache[page, 0], NT, preferred_element_type=F32
-            )
-        return 0
-
-    lax.fori_loop(0, N, local_scores, 0, unroll=8)
-
-    cp_tsm.wait()
-    for dy in (0, 1, 3, 2):
-        row = lax.rem(y0 + 4 - dy, 4)
-        at = pl.ds(pl.multiple_of(row * 128, 128), 128)
-        drain(qrecv, HEADS, gsem.at[dy], 7 if dy == 0 else 8)
-        q = spread_heads(qrecv[at, :])
-        pages = [jnp.clip(tsm[row * 8 + i, 1], 0, PAGE - 1) for i in range(8)]
-        s = jnp.concatenate(
-            [
-                lax.dot_general(
-                    q[i * HEADS : (i + 1) * HEADS],
-                    cache[pages[i], 0],
-                    NT,
-                    preferred_element_type=F32,
-                )
-                for i in range(8)
-            ],
-            axis=0,
-        )
-        s = s * SCALE + sbias[at, :]
-        m = jnp.max(s, axis=1, keepdims=True)
-        w = jnp.exp(s - m)
-        total = jnp.sum(w, axis=1, keepdims=True)
-        w = w.astype(BF)
-        o = jnp.concatenate(
-            [dot(w[i * HEADS : (i + 1) * HEADS], cache[pages[i], 1]) for i in range(8)], axis=0
-        )
-        psend[at, :] = (block_select(o[:, :HD], o[:, HD:], 128) / total).astype(BF)
-        lse = jnp.where(
-            iota((128, 128), 1) == (iota((128, 128), 0) & 15), m + jnp.log(total), 0.0
-        )
-        lsend[pl.ds(pl.multiple_of(row * 8, 8), 8), :] = jnp.sum(
-            lse.reshape(8, HEADS, 128), axis=1
-        )
-        back = (4 - dy) % 4
-        peers(back, sender(lsend, lrecv, 1, ssem.at[6], rsem.at[6]))
-        peers(back, sender(psend, precv, HEADS, ssem.at[5], rsem.at[5]))
-    keep(lsend, lrecv, 1)
-    keep(psend, precv, HEADS)
-
-    def local_weights(b, _):
-        at = rows_of(b)
+        sl[at, :] = dot(qbd[at, :], kt[r])
+        return 0
+
+
+    def local_weights(b):
+        at = slice(b * 256, (b + 1) * 256)
         new = loc[at, 0:1]
         parts = [
             sl[at, j * PAGE : (j + 1) * PAGE] * SCALE + lbias[at, j * PAGE : (j + 1) * PAGE]
@@ -381,18 +368,67 @@
         m = jnp.maximum(jnp.maximum(parts[0], parts[1]), jnp.maximum(parts[2], parts[3]))
         m = jnp.maximum(jnp.max(m, axis=1, keepdims=True), new)
         wf = jnp.exp(new - m)
-        total = jnp.zeros((blk, PAGE), F32)
+        total = jnp.zeros((256, PAGE), F32)
         for j in range(MAXP):
             w = jnp.exp(parts[j] - m)
             total += w
             wl[at, j * PAGE : (j + 1) * PAGE] = w.astype(BF)
         total = jnp.sum(total, axis=1, keepdims=True) + wf
-        at_lane = iota((blk, 128), 1)
+        at_lane = iota((256, 128), 1)
         stat = jnp.where(at_lane == 0, m, jnp.where(at_lane == 1, total, 0.0))
         loc[at, :] = jnp.where(at_lane == 2, wf, stat)
-        return 0
-
-    lax.fori_loop(0, ROWS // blk, local_weights, 0)
+
+    def serve(*hops):
+        slots = [d0] if 0 in hops else []
+        for dist in hops:
+            near = [
+                rows8[dy] + around[dx][dc]
+                for dy in range(4)
+                for dx in range(4)
+                for dc in range(2)
+                if FAR[dy] + FAR[dx] == dist and (dy, dx, dc) != (0, 0, 0)
+            ]
+            drain(qrecv, HEADS, gsem.at[dist], len(near))
+            slots += near
+        n = len(slots) * HEADS
+        ats = [pl.ds(pl.multiple_of(slot * HEADS, HEADS), HEADS) for slot in slots]
+        s = [dot(spread_heads(qrecv[at, :]), kts[slot]) for at, slot in zip(ats, slots)]
+        bias = jnp.concatenate([sbias[at, :] for at in ats], axis=0)
+        s = jnp.concatenate(s, axis=0) * SCALE + bias
+        m = jnp.max(s, axis=1, keepdims=True)
+        w = jnp.exp(s - m)
+        total = jnp.sum(w, axis=1, keepdims=True)
+        w = w.astype(BF)
+        o = [
+            dot(
+                w[i * HEADS : (i + 1) * HEADS],
+                cache[jnp.clip(tsm[slot, 1], 0, PAGE - 1), 1],
+            )
+            for i, slot in enumerate(slots)
+        ]
+        o = jnp.concatenate(o, axis=0)
+        o = (block_select(o[:, :HD], o[:, HD:], n) / total).astype(BF)
+        lse = jnp.where(
+            iota((n, 128), 1) == (iota((n, 128), 0) & 15), m + jnp.log(total), 0.0
+        )
+        lse = jnp.sum(lse.reshape(n // HEADS, HEADS, 128), axis=1)
+        for i, slot in enumerate(slots):
+            lsend[pl.ds(slot, 1), :] = lse[i : i + 1]
+            psend[ats[i], :] = o[i * HEADS : (i + 1) * HEADS]
+        for slot in slots[1 if 0 in hops else 0 :]:
+            sender(lsend, lrecv, 1, ssem.at[6], rsem.at[6])(slot, None)
+            sender(psend, precv, HEADS, ssem.at[5], rsem.at[5])(slot, None)
+
+    lax.fori_loop(0, N // 2, local_scores, 0, unroll=8)
+    serve(0, 1, 2)
+    serve(3)
+    serve(4)
+    keep(lsend, lrecv, 1)
+    keep(psend, precv, HEADS)
+
+    lax.fori_loop(N // 2, N, local_scores, 0, unroll=8)
+    local_weights(0)
+    local_weights(1)
 
     def local_values(r, _):
         at = pl.ds(pl.multiple_of(r * HEADS, HEADS), HEADS)
@@ -418,7 +454,7 @@
         locp[at, HD:] = stat.astype(BF)
         return 0
 
-    lax.fori_loop(0, ROWS // blk, local_part, 0)
+    lax.fori_loop(0, ROWS // blk, local_part, 0, unroll=4)
     mine = dot(ph[...], locp[...])
     ol[...] = mine[:, :HD]
     loc[...] = jnp.broadcast_to(
@@ -490,6 +526,8 @@
             v((CW, width), BF),
             v((CW, width), BF),
             v((PAGE, 2, PAGE, CW), BF),
+            v((N, CW, MAXP * PAGE), BF),
+            v((N, CW, PAGE), BF),
             v((ROWS, CW), BF),
             v((ROWS, CW), BF),
             v((ROWS, CW), BF),
@@ -504,15 +542,14 @@
             v((ROWS, HD), BF),
             v((N, 128), F32),
             v((N, 128), F32),
+            v((128, 128), BF),
             v((ROWS, ROWS), BF),
-            v((ROWS, ROWS), BF),
-            v((ROWS, ROWS), BF),
-            v((CW, ROWS), BF),
             v((2 * ROWS, ROWS), BF),
             v((ROWS, N), BF),
             v((ROWS, 128), F32),
             v((ROWS, CW), BF),
-            v((ROWS, HD), BF),
+            v((ROWS, HD), F32),
+            v((ROWS, HD), F32),
             v((ROWS, CW), BF),
             v((ROWS, CW), F32),
             v((ROWS, ROWS), F32),
@@ -526,7 +563,7 @@
             pltpu.SemaphoreType.DMA((14,)),
             pltpu.SemaphoreType.DMA((7,)),
             pltpu.SemaphoreType.DMA((7,)),
-            pltpu.SemaphoreType.DMA((4,)),
+            pltpu.SemaphoreType.DMA((5,)),
         ],
         compiler_params=pltpu.CompilerParams(
             collective_id=0, has_side_effects=True, vmem_limit_bytes=63 * 1024 * 1024

time: 41.4 us -> 39.5 us (0.954)
  Pallas kernels: 39.7 us -> 37.8 us
    pallas_call x1, Pallas kernels: 39.7 us -> 37.8 us  [shards(): pl.pallas_call(kernel, out_shape=jax.ShapeDtypeStruct((N, width), BF), in...]
where the time goes in v3:
time: 39.5 us; the launch traced here: 39.4 us
  Pallas kernels  37.8 us (96%)
  local copies, waits for them, and re-layouts  1.57 us (4%)
    pallas_call x1, Pallas kernels, shards(): pl.pallas_call(kernel, out_shape=jax.ShapeDtypeStruct((N, width), BF), in...  37.8 us
    unnamed x1, local copies, waits for them, and re-layouts  1.57 us

profile of v3, /device:TPU:1, one launch (start us, length us, event | category | flops | bytes accessed | tf_op | source)
XLA Modules:
  0.0 39.4 jit_solution(3421097001147251075)
XLA Ops:
  0.0 37.8 %shard_map.118 = bf16[32,2048]{1,0:T(8,128)(2,1)} custom-call(s32[1,32]{1,0:T(1,128)} %bitcast.10, s32[1,32]{1,0:T(1,128)} %fetch_hbm.1, s32[4,32]{1,0:T(4,128)} %bitcast.8, s32[1,32]{1,0:T(1,128)} %move_hbm.1, s32[4,32]{1,0:T(4,128)} %bitcast.9, s32[1,32]{1,0:T(1,128)} %bitcast.11, bf16[32,2,256]{2,1,0:T(2,128)(2,1)} %fresh_hbm.1, ...), custom_call_target="tpu_custom_call" | custom-call | tf_op jit(solution)/shard_map/pallas_call | solution.py:510
  37.8 1.6 %copy.14 = bf16[32,2048]{1,0:T(8,128)(2,1)} copy(bf16[32,2048]{1,0:T(8,128)(2,1)} %shard_map.118) | data formatting | bytes 262144

commit v4 on v3

--- a/solution.py
+++ b/solution.py
@@ -43,6 +43,10 @@
     hi = x.astype(BF).astype(F32)
     mid = (x - hi).astype(BF).astype(F32)
     return hi, mid, x - hi - mid
+
+
+def swap(x):
+    return jnp.concatenate([x[:, RANK:], x[:, :RANK]], axis=1)
 
 
 def block_select(left, right, rows):
@@ -249,7 +253,14 @@
     )
     wanted = (iota((2 * N, CW), 1) >> 6).astype(F32) == adapter
     acc = jnp.where(wanted, acc, 0.0)
-    zbuf[pl.ds(z0, 1)] = (acc[:, :128] + acc[:, 128:])[None]
+    acc = acc[:, :128] + acc[:, 128:]
+    acc = acc + swap(acc)
+    first_half = iota((N, 128), 1) < RANK
+    zbuf[pl.ds(z0, 1)] = jnp.where(
+        first_half,
+        jnp.concatenate([acc[g * 16 : g * 16 + 8] for g in range(4)], axis=0),
+        jnp.concatenate([acc[g * 16 + 8 : g * 16 + 16] for g in range(4)], axis=0),
+    )[None]
     for k in (2, 1, 3):
         pltpu.make_async_remote_copy(
             src_ref=zbuf.at[z0],
@@ -271,6 +282,9 @@
     cp_up.wait()
     pltpu.make_async_copy(zpart, zpart, rsem.at[2]).wait()
     u = (zbuf[0] + zbuf[1]) + (zbuf[2] + zbuf[3])
+    turned = swap(u)
+    slots = [jnp.where(first_half, u, turned), jnp.where(first_half, turned, u)]
+    u = jnp.concatenate([slots[s][g * 8 : (g + 1) * 8] for g in range(4) for s in (0, 1)], axis=0)
     u = jnp.where(wanted, jnp.concatenate([u, u], axis=1), 0.0).astype(BF)
     deltas = [dot(u, up[:, c * CW : (c + 1) * CW]).astype(BF) for c in range(CH)]
     for g in range(4):
@@ -421,8 +435,8 @@
 
     lax.fori_loop(0, N // 2, local_scores, 0, unroll=8)
     serve(0, 1, 2)
+    serve(4)
     serve(3)
-    serve(4)
     keep(lsend, lrecv, 1)
     keep(psend, precv, HEADS)
 
@@ -535,7 +549,7 @@
             v((N, 128), I32),
             v((N, 128), I32),
             pltpu.SMEM((N, 128), I32),
-            v((Z, 2 * N, 128), F32),
+            v((Z, N, 128), F32),
             v((ROWS, HD), BF),
             v((ROWS, HD), BF),
             v((ROWS, HD), BF),

time: 39.5 us -> 39.2 us (level)
  no operation moved by 1% of the time
where the time goes in v4:
time: 39.2 us; the launch traced here: 39.1 us
  Pallas kernels  37.5 us (96%)
  local copies, waits for them, and re-layouts  1.57 us (4%)
    pallas_call x1, Pallas kernels, shards(): pl.pallas_call(kernel, out_shape=jax.ShapeDtypeStruct((N, width), BF), in...  37.5 us
    unnamed x1, local copies, waits for them, and re-layouts  1.57 us

profile of v4, /device:TPU:1, one launch (start us, length us, event | category | flops | bytes accessed | tf_op | source)
XLA Modules:
  0.0 39.1 jit_solution(10416491779324432427)
XLA Ops:
  0.0 37.5 %shard_map.118 = bf16[32,2048]{1,0:T(8,128)(2,1)} custom-call(s32[1,32]{1,0:T(1,128)} %bitcast.10, s32[1,32]{1,0:T(1,128)} %fetch_hbm.1, s32[4,32]{1,0:T(4,128)} %bitcast.8, s32[1,32]{1,0:T(1,128)} %move_hbm.1, s32[4,32]{1,0:T(4,128)} %bitcast.9, s32[1,32]{1,0:T(1,128)} %bitcast.11, bf16[32,2,256]{2,1,0:T(2,128)(2,1)} %fresh_hbm.1, ...), custom_call_target="tpu_custom_call" | custom-call | tf_op jit(solution)/shard_map/pallas_call | solution.py:524
  37.5 1.6 %copy.14 = bf16[32,2048]{1,0:T(8,128)(2,1)} copy(bf16[32,2048]{1,0:T(8,128)(2,1)} %shard_map.118) | data formatting | bytes 262144

commit v5 on v4

--- a/solution.py
+++ b/solution.py
@@ -59,7 +59,7 @@
     hid_hbm, base_hbm, down_hbm, up_hbm, cache_hbm,
     out_ref,
     own_ref, fetch_ref, tab_ref, move_ref, mask_ref, len_ref, fresh_ref, tab_s,
-    hid, base, down, up, cache, kt, kts,
+    outv, hid, base, down, up, cache, kt, kts,
     hsend, hrecv, dsend, drecv, tsend, trecv, tsm, zbuf,
     qsend, qrecv, psend, precv, lsend, lrecv,
     turn, ph, qsel, ex, cx, st1, basep, basel,
@@ -477,21 +477,27 @@
 
     drain(lrecv, 1, rsem.at[6])
     stats = jnp.transpose(lrecv[...])
+    shares = []
+    for g in range(4):
+        mine = loc[g * 128 : (g + 1) * 128, :]
+        row = jnp.concatenate([stats[4 * g + i : 4 * g + i + 1, :] for i in range(4)], axis=1)
+        lse = row + mbias[...]
+        top = jnp.maximum(jnp.max(lse, axis=1, keepdims=True), mine)
+        shares.append((jnp.exp(lse - top).astype(BF), jnp.exp(mine - top)))
     drain(precv, HEADS, rsem.at[5])
     others = dot(ph[...], precv[...]).astype(BF)
     others = jnp.concatenate([others, jnp.ones((ROWS, 128), BF)], axis=1)
-    for g in range(4):
+    results = []
+    for g, (w, wm) in enumerate(shares):
         at = slice(g * 128, (g + 1) * 128)
-        row = jnp.concatenate([stats[4 * g + i : 4 * g + i + 1, :] for i in range(4)], axis=1)
-        lse = row + mbias[...]
-        mine = loc[at, :]
-        top = jnp.maximum(jnp.max(lse, axis=1, keepdims=True), mine)
-        both = dot(jnp.exp(lse - top).astype(BF), others[at])
-        wm = jnp.exp(mine - top)
+        both = dot(w, others[at])
         o = (both[:, :HD] + wm * ol[at, :]) / (both[:, HD:] + wm)
         for i in range(4):
             h = 4 * g + i
-            out_ref[:, h * HD : (h + 1) * HD] = o[i * N : (i + 1) * N].astype(BF)
+            outv[:, h * HD : (h + 1) * HD] = o[i * N : (i + 1) * N].astype(BF)
+        part = pl.ds(g * 4 * HD, 4 * HD)
+        results.append(pltpu.make_async_copy(outv.at[:, part], out_ref.at[:, part], lsem.at[14 + g]))
+        results[-1].start()
 
     drain(hsend, HEADS, ssem.at[0])
     drain(tsend, 1, ssem.at[1])
@@ -500,6 +506,8 @@
     drain(qsend, HEADS, ssem.at[4])
     drain(psend, HEADS, ssem.at[5])
     drain(lsend, 1, ssem.at[6])
+    for cp in results:
+        cp.wait()
 
 
 def shards(
@@ -518,14 +526,13 @@
 ):
     width = N * 64
     table = request_page_table.T
-    vmem = pl.BlockSpec(memory_space=pltpu.VMEM)
     hbm = pl.BlockSpec(memory_space=pltpu.HBM)
     v = pltpu.VMEM
     return pl.pallas_call(
         kernel,
         out_shape=jax.ShapeDtypeStruct((N, width), BF),
         in_specs=[hbm] * 12,
-        out_specs=vmem,
+        out_specs=hbm,
         scratch_shapes=[
             v((1, N), I32),
             v((1, N), I32),
@@ -535,6 +542,7 @@
             v((1, N), I32),
             v((N, 2, CW), BF),
             pltpu.SMEM((MAXP, N), I32),
+            v((N, width), BF),
             v((N, width), BF),
             v((N, width), BF),
             v((CW, width), BF),
@@ -574,7 +582,7 @@
             v((ROWS, HD), F32),
             v((ROWS, 128), F32),
             v((ROWS, CW), BF),
-            pltpu.SemaphoreType.DMA((14,)),
+            pltpu.SemaphoreType.DMA((18,)),
             pltpu.SemaphoreType.DMA((7,)),
             pltpu.SemaphoreType.DMA((7,)),
             pltpu.SemaphoreType.DMA((5,)),

time: 39.2 us -> 39.4 us (level)
  no operation moved by 1% of the time
where the time goes in v5:
time: 39.4 us; the launch traced here: 39.3 us
  Pallas kernels  37.7 us (96%)
  local copies, waits for them, and re-layouts  1.57 us (4%)
    pallas_call x1, Pallas kernels, shards(): pl.pallas_call(kernel, out_shape=jax.ShapeDtypeStruct((N, width), BF), in...  37.7 us
    unnamed x1, local copies, waits for them, and re-layouts  1.57 us

profile of v5, /device:TPU:1, one launch (start us, length us, event | category | flops | bytes accessed | tf_op | source)
XLA Modules:
  0.0 39.3 jit_solution(405294094278871854)
XLA Ops:
  0.0 37.7 %shard_map.118 = bf16[32,2048]{1,0:T(8,128)(2,1)} custom-call(s32[1,32]{1,0:T(1,128)} %bitcast.10, s32[1,32]{1,0:T(1,128)} %fetch_hbm.1, s32[4,32]{1,0:T(4,128)} %bitcast.8, s32[1,32]{1,0:T(1,128)} %move_hbm.1, s32[4,32]{1,0:T(4,128)} %bitcast.9, s32[1,32]{1,0:T(1,128)} %bitcast.11, bf16[32,2,256]{2,1,0:T(2,128)(2,1)} %fresh_hbm.1, ...), custom_call_target="tpu_custom_call" | custom-call | tf_op jit(solution)/shard_map/pallas_call | solution.py:531
  37.7 1.6 %copy.14 = bf16[32,2048]{1,0:T(8,128)(2,1)} copy(bf16[32,2048]{1,0:T(8,128)(2,1)} %shard_map.118) | data formatting | bytes 262144
